TPU v7x, 32 devices: a whole 2x2x4 slice. The times are simulated.
32 devices in a mesh: dp: 4 (over x, core), seq: 8 (over z, y).
Axes of the slice: x: 2, y: 2, z: 4, core: 2. Of those that a mesh axis runs over, the one named last changes fastest.
Arguments:
- activations: bfloat16 [4, 1024, 768], P('dp', 'seq'), may hold values from -600 to 600
- conv_weight: bfloat16 [3840, 768], replicated, may hold values from -0.09375 to 0.09375
- head_first: bfloat16 [768, 768], replicated, may hold values from -0.21875 to 0.21875
- head_second: bfloat16 [768], replicated, may hold values from -5 to 5
- hidden_cotangent: bfloat16 [4, 1024, 768], P('dp', 'seq'), may hold values from -3 to 3
- score_cotangent: float32 [4, 1024], P('dp', 'seq'), may hold values from -5 to 5
- donor_row: int32 [4, 1024], P('dp', 'seq'), may hold values from 0 to 127
- acceptor_owner: int32 [4, 1024, 1], P('dp', 'seq'), may hold values from 0 to 7; in each aligned block of 128 rows (0 to 127, 128 to 255, ..., all dimensions but the last counted through in order) at most 32 rows name the same one
- acceptor_row: int32 [4, 1024], P('dp', 'seq'), may hold values from 0 to 127
Outputs:
- input_grad: bfloat16 [4, 1024, 768], P('dp', 'seq')
- weight_grads: float32 [4608, 768], P('seq', 'dp')
Inputs may be any that keep to these rules, and one draw needn't show every extreme that they name: `acceptor_owner`: among the 128 pairs of one block of positions, no block index is named by more than 32 pairs, a bound that some block reaches in every draw.
All inputs are finite; a program needn't handle non-finite values.
Results may differ from a plain program's by a relative error of at most 0.01.
Values may be sent and summed in bfloat16 or wider, within the bound.
A program may use at most 64 MiB of HBM per device.

v0:
```python
import math

import jax
import jax.numpy as jnp
from jax import lax
from jax.sharding import PartitionSpec as P

DILATION = 8


def with_halo(cells, sides, width):
    for axis, dim in sides:
        count = lax.axis_size(axis)
        ends = count - 1
        head = lax.slice_in_dim(cells, 0, width, axis=dim)
        tail = lax.slice_in_dim(cells, cells.shape[dim] - width, cells.shape[dim], axis=dim)
        cells = jnp.concatenate(
            [
                lax.ppermute(tail, axis, [(i, (i + 1) % count) for i in range(ends)]),
                cells,
                lax.ppermute(head, axis, [((i + 1) % count, i) for i in range(ends)]),
            ],
            axis=dim,
        )
    return cells


def gelu_slope(values):
    normal_cdf = 0.5 * (1.0 + lax.erf(values * (1.0 / math.sqrt(2.0))))
    density = jnp.exp(-0.5 * values * values) * (1.0 / math.sqrt(2.0 * math.pi))
    return normal_cdf + values * density


def contract_rows(left_side, right_side):
    return lax.dot_general(
        left_side, right_side, (((0,), (0,)), ((), ())), preferred_element_type=jnp.float32
    )


def widened(field, reach_rows):
    return with_halo(field, (("seq", 0),), reach_rows)


def per_device(
    activations,
    conv_weight,
    head_first,
    head_second,
    hidden_cotangent,
    score_cotangent,
    donor_row,
    acceptor_owner,
    acceptor_row,
):
    row_count = activations.shape[1]
    chan_count = activations.shape[2]
    out_count = conv_weight.shape[1]
    tap_count = conv_weight.shape[0] // chan_count
    reach_rows = (tap_count - 1) // 2 * DILATION
    shards = lax.axis_size("seq")
    batch_total = lax.axis_size("dp") * activations.shape[0]
    pair_count = donor_row.shape[1]
    capacity = max(2, 2 * pair_count // shards)
    input_values = activations[0].astype(jnp.float32)
    norm_inverse = lax.rsqrt(jnp.mean(input_values * input_values, axis=1, keepdims=True) + 1e-05)
    normed = (input_values * norm_inverse).astype(jnp.bfloat16)
    padded = widened(normed, reach_rows)
    columns = jnp.concatenate(
        [
            padded[tap_index * DILATION : tap_index * DILATION + row_count]
            for tap_index in range(tap_count)
        ],
        axis=1,
    )
    preact = jnp.dot(columns, conv_weight, preferred_element_type=jnp.float32)
    hidden = jax.nn.gelu(preact, approximate=False).astype(jnp.bfloat16)
    owner_index = acceptor_owner[0, :, 0]
    owner_hits = (owner_index[:, None] == jnp.arange(shards, dtype=jnp.int32)[None, :]).astype(
        jnp.int32
    )
    earlier = jnp.cumsum(owner_hits, axis=0) - owner_hits
    slot_index = jnp.sum(earlier * owner_hits, axis=1)
    target = owner_index * capacity + slot_index
    request = (
        jnp.full((shards * capacity,), -1, jnp.int32)
        .at[target]
        .set(acceptor_row[0])
        .reshape(shards, capacity)
    )
    asked_rows = lax.all_to_all(request, "seq", split_axis=0, concat_axis=0, tiled=True)
    picked = jnp.take(hidden, jnp.maximum(asked_rows, 0), axis=0)
    returned = lax.all_to_all(picked, "seq", split_axis=0, concat_axis=0, tiled=True)
    accept_feat = returned.reshape(shards * capacity, out_count)[target]
    donor_feat = hidden[donor_row[0]]
    accept_values = accept_feat.astype(jnp.float32)
    donor_values = donor_feat.astype(jnp.float32)
    pair_feature = (donor_values * accept_values).astype(jnp.bfloat16)
    head_preact = jnp.dot(pair_feature, head_first, preferred_element_type=jnp.float32)
    head_delta = (
        score_cotangent[0][:, None]
        * head_second.astype(jnp.float32)[None, :]
        * gelu_slope(head_preact)
    ).astype(jnp.bfloat16)
    feature_grad = lax.dot_general(
        head_delta, head_first, (((1,), (1,)), ((), ())), preferred_element_type=jnp.float32
    )
    donor_grad = (feature_grad * accept_values).astype(jnp.bfloat16)
    accept_grad = (feature_grad * donor_values).astype(jnp.bfloat16)
    outgoing = (
        jnp.zeros((shards * capacity, out_count), jnp.bfloat16)
        .at[target]
        .set(accept_grad)
        .reshape(shards, capacity, out_count)
    )
    incoming = lax.all_to_all(outgoing, "seq", split_axis=0, concat_axis=0, tiled=True)
    row_ids = jnp.arange(row_count, dtype=jnp.int32)
    accept_hits = (asked_rows.reshape(-1)[:, None] == row_ids[None, :]).astype(jnp.bfloat16)
    donor_hits = (donor_row[0][:, None] == row_ids[None, :]).astype(jnp.bfloat16)
    hidden_grad = hidden_cotangent[0].astype(jnp.float32) + contract_rows(donor_hits, donor_grad)
    hidden_grad = hidden_grad + contract_rows(
        accept_hits, incoming.reshape(shards * capacity, out_count)
    )
    preact_grad = (hidden_grad * gelu_slope(preact)).astype(jnp.bfloat16)
    grad_padded = widened(preact_grad, reach_rows)
    spread = lax.dot_general(
        grad_padded, conv_weight, (((1,), (1,)), ((), ())), preferred_element_type=jnp.float32
    )
    normed_grad = spread[2 * reach_rows : 2 * reach_rows + row_count, 0:chan_count]
    for tap_index in range(1, tap_count):
        first_row = 2 * reach_rows - tap_index * DILATION
        normed_grad = (
            normed_grad
            + spread[
                first_row : first_row + row_count,
                tap_index * chan_count : (tap_index + 1) * chan_count,
            ]
        )
    input_grad = norm_inverse * normed_grad - input_values * norm_inverse**3 * jnp.mean(
        normed_grad * input_values, axis=1, keepdims=True
    )
    conv_term = contract_rows(columns, preact_grad) * (
        1.0 / math.sqrt(batch_total * row_count * shards)
    )
    head_term = contract_rows(pair_feature, head_delta) * (
        1.0 / math.sqrt(batch_total * pair_count * shards)
    )
    grad_term = jnp.concatenate([conv_term, head_term], axis=0)
    column_share = lax.psum_scatter(
        grad_term.astype(jnp.bfloat16), "dp", scatter_dimension=1, tiled=True
    ).astype(jnp.float32)
    weight_grads = lax.psum_scatter(column_share, "seq", scatter_dimension=0, tiled=True)
    return (input_grad.astype(jnp.bfloat16)[None], weight_grads)


def solution(mesh):
    placed = (
        P("dp", "seq", None),
        P(),
        P(),
        P(),
        P("dp", "seq", None),
        P("dp", "seq"),
        P("dp", "seq"),
        P("dp", "seq", None),
        P("dp", "seq"),
    )
    return jax.shard_map(
        per_device,
        mesh=mesh,
        in_specs=placed,
        out_specs=(P("dp", "seq", None), P("seq", "dp")),
        check_vma=False,
    )
```

profile of v0, /device:TPU:26, one launch (start us, length us, event | category | flops | bytes accessed | tf_op | source)
XLA Modules:
  0.0 263.8 jit_solution(15146860900753645235)
XLA Ops:
  7.2 0.8 fusion.54
  8.0 0.2 reduce_window_sum.11
  8.2 0.8 select_reduce_fusion
  9.0 0.7 fusion.57
  9.7 1.1 scatter_custom_fusion
  10.8 0.7 all_to_all.12
  11.5 6.1 %all-to-all-start = ((s32[8,1,32]{2,1,0:T(1,128)}), s32[8,1,32]{2,1,0:T(1,128)S(1)}, u32[]{:S(2)}, u32[]{:S(2)}) async-start(s32[8,1,32]{2,1,0:T(1,128)} %all_to_all.12), calls=%async_computation | async-start | bytes 8192 | tf_op jit(solution)/shard_map/all_to_all | solution.py:90
  17.5 1.0 fusion.18
  18.6 1.0 fusion.19
  19.6 3.4 %collective-permute-start.1 = (bf16[16,768]{1,0:T(8,128)(2,1)S(1)}, bf16[16,768]{1,0:T(8,128)(2,1)S(1)}, u32[]{:S(2)}, u32[]{:S(2)}) collective-permute-start(bf16[16,768]{1,0:T(8,128)(2,1)S(1)} %get-tuple-element.12), channel_id=1, source_target_pairs={{1,0},{2,1},{3,2},{4,3},{5,4},{6,5},{7,6},{9,8},{10,9},{11,10},{12... | collective-permute-start | bytes 73736 | tf_op jit(solution)/shard_map/ppermute | solution.py:21
  23.0 2.5 collective-permute-start
  25.5 0.1 reshape.138
  25.6 4.0 %collective-permute-done = bf16[16,768]{1,0:T(8,128)(2,1)S(1)} collective-permute-done((bf16[16,768]{1,0:T(8,128)(2,1)S(1)}, bf16[16,768]{1,0:T(8,128)(2,1)S(1)}, u32[]{:S(2)}, u32[]{:S(2)}) %collective-permute-start) | collective-permute-done | bytes 24608 | tf_op jit(solution)/shard_map/ppermute | solution.py:19
  29.7 1.0 constant_dynamic-update-slice_fusion
  30.8 5.1 %fusion.7 = (bf16[128,768]{1,0:T(8,128)(2,1)S(1)}, f32[128,768]{1,0:T(8,128)}) fusion(bf16[128,3840]{1,0:T(8,128)(2,1)S(1)} %fusion.45, bf16[3840,768]{1,0:T(8,128)(2,1)} %param.10), kind=kOutput, calls=%fused_computation.27 | convolution fusion | flops 761364480 | bytes 7471104 | tf_op jit(solution)/shard_map/dot_general | solution.py:75
  35.9 1.2 gather_fusion.1
  37.1 0.8 broadcast_select_fusion
  37.9 5.1 %all-to-all-start.1 = ((bf16[8,32,768]{2,1,0:T(8,128)(2,1)}), bf16[8,32,768]{2,1,0:T(8,128)(2,1)S(1)}, u32[]{:S(2)}, u32[]{:S(2)}) async-start(bf16[8,32,768]{2,1,0:T(8,128)(2,1)} %broadcast_select_fusion), calls=%async_computation.1 | async-start | bytes 786432 | tf_op jit(solution)/shard_map/all_to_all | solution.py:92
  43.1 0.9 gather_fusion
  44.0 6.1 %all-to-all-done.1 = bf16[8,32,768]{2,1,0:T(8,128)(2,1)S(1)} async-done(((bf16[8,32,768]{2,1,0:T(8,128)(2,1)}), bf16[8,32,768]{2,1,0:T(8,128)(2,1)S(1)}, u32[]{:S(2)}, u32[]{:S(2)}) %all-to-all-start.1) | async-done | bytes 393248 | tf_op jit(solution)/shard_map/all_to_all | solution.py:92
  50.1 0.9 gather_fusion.2
  51.0 0.4 fusion.13
  51.4 0.5 fusion.63
  51.9 1.9 scatter_custom_fusion.1
  53.8 6.6 %all-to-all-start.2 = ((bf16[8,32,768]{2,1,0:T(8,128)(2,1)}), bf16[8,32,768]{2,1,0:T(8,128)(2,1)}, u32[]{:S(2)}, u32[]{:S(2)}) async-start(bf16[8,32,768]{2,1,0:T(8,128)(2,1)} %bitcast.16), calls=%async_computation.2 | async-start | bytes 786432 | tf_op jit(solution)/shard_map/all_to_all | solution.py:115
  60.5 0.5 broadcast.156
  61.0 0.6 reduce.3
  61.6 0.1 eq.53
  61.6 1.1 convolution_add_fusion.1
  62.7 1.5 multiply_convert_fusion.1
  64.2 4.0 %all-to-all-done.2 = bf16[8,32,768]{2,1,0:T(8,128)(2,1)} async-done(((bf16[8,32,768]{2,1,0:T(8,128)(2,1)}), bf16[8,32,768]{2,1,0:T(8,128)(2,1)}, u32[]{:S(2)}, u32[]{:S(2)}) %all-to-all-start.2) | async-done | bytes 393248 | tf_op jit(solution)/shard_map/all_to_all | solution.py:115
  68.3 1.6 fusion.1
  69.9 4.2 %multiply_convert_fusion = bf16[3840,768]{1,0:T(8,128)(2,1)} fusion(bf16[128,3840]{1,0:T(8,128)(2,1)S(1)} %fusion.45, bf16[128,768]{1,0:T(8,128)(2,1)S(1)} %fusion.1), kind=kOutput, calls=%fused_computation.5 | convolution fusion | flops 760872960 | bytes 7077888 | tf_op jit(solution)/shard_map/dot_general | solution.py:35
  74.1 6.0 %pad_maximum_fusion = bf16[4608,768]{1,0:T(8,128)(2,1)} fusion(bf16[768,768]{1,0:T(8,128)(2,1)S(1)} %multiply_convert_fusion.1, bf16[3840,768]{1,0:T(8,128)(2,1)} %multiply_convert_fusion), kind=kLoop, calls=%fused_computation.6 | loop fusion | flops 14155776 | bytes 14155776 | tf_op jit(solution)/shard_map/concatenate | solution.py:147
  80.1 10.2 %copy.15 = bf16[4608,768]{0,1:T(8,128)(2,1)} copy(bf16[4608,768]{1,0:T(8,128)(2,1)} %pad_maximum_fusion) | data formatting | bytes 14155776
  90.3 0.0 reduce-scatter.5.cloned.1.call-start
  90.4 64.1 %reduce-scatter.7.cloned.1.call-done = bf16[192,4608]{1,0:T(8,128)(2,1)} async-done(((bf16[768,4608]{1,0:T(8,128)(2,1)}), bf16[192,4608]{1,0:T(8,128)(2,1)}) %reduce-scatter.7.cloned.1.call-update) | async-done | bytes 1769488
  154.5 2.7 %copy.16 = bf16[4608,192]{1,0:T(8,128)(2,1)S(1)} copy(bf16[4608,192]{0,1:T(8,128)(2,1)} %bitcast.54) | data formatting | bytes 3538944
  157.2 2.5 convert_element_type.70
  159.7 0.8 fusion.61
  160.5 3.4 %collective-permute-start.2 = (bf16[16,768]{1,0:T(8,128)(2,1)S(1)}, bf16[16,768]{1,0:T(8,128)(2,1)S(1)}, u32[]{:S(2)}, u32[]{:S(2)}) collective-permute-start(bf16[16,768]{1,0:T(8,128)(2,1)S(1)} %get-tuple-element.10), channel_id=1, source_target_pairs={{0,1},{1,2},{2,3},{3,4},{4,5},{5,6},{6,7},{8,9},{9,10},{10,11},{11... | collective-permute-start | bytes 73736 | tf_op jit(solution)/shard_map/ppermute | solution.py:19
  163.9 3.4 %collective-permute-start.3 = (bf16[16,768]{1,0:T(8,128)(2,1)S(1)}, bf16[16,768]{1,0:T(8,128)(2,1)S(1)}, u32[]{:S(2)}, u32[]{:S(2)}) collective-permute-start(bf16[16,768]{1,0:T(8,128)(2,1)S(1)} %get-tuple-element.11), channel_id=1, source_target_pairs={{1,0},{2,1},{3,2},{4,3},{5,4},{6,5},{7,6},{9,8},{10,9},{11,10},{12... | collective-permute-start | bytes 73736 | tf_op jit(solution)/shard_map/ppermute | solution.py:21
  167.3 2.3 collective-permute-done.3
  169.6 4.9 %fusion.31 = f32[160,3840]{1,0:T(8,128)S(1)} fusion(bf16[3840,768]{1,0:T(8,128)(2,1)} %param.10, bf16[16,768]{1,0:T(8,128)(2,1)S(1)} %collective-permute-done.3, bf16[128,768]{1,0:T(8,128)(2,1)} %copy-done.3, bf16[16,768]{1,0:T(8,128)(2,1)S(1)} %collective-permute-done.2), kind=kOutput, calls=%fused_computation.64 | convolution fusion | flops 944455680 | bytes 8601600 | tf_op jit(solution)/shard_map/dot_general | solution.py:125
  174.5 0.2 fusion.23
  174.7 0.8 fusion.41
  175.5 79.3 %reduce-scatter.5.cloned.1.call-done = f32[576,192]{1,0:T(8,128)} async-done(((f32[4608,192]{1,0:T(8,128)}), f32[576,192]{1,0:T(8,128)}) %reduce-scatter.5.cloned.1.call-update) | async-done | bytes 442384 | tf_op jit(solution)/shard_map/reduce_scatter | solution.py:151
  254.9 2.1 copy.14
  (38 shorter events, 0.2 us)
Async XLA Ops:
  7.2 43.8 %copy-start = (bf16[768,768]{1,0:T(8,128)(2,1)S(1)}, bf16[768,768]{1,0:T(8,128)(2,1)}, u32[]{:S(2)}) copy-start(bf16[768,768]{1,0:T(8,128)(2,1)} %param.11) | copy-start | bytes 3538948
  11.5 14.0 %all-to-all-start = ((s32[8,1,32]{2,1,0:T(1,128)}), s32[8,1,32]{2,1,0:T(1,128)S(1)}, u32[]{:S(2)}, u32[]{:S(2)}) async-start(s32[8,1,32]{2,1,0:T(1,128)} %all_to_all.12), calls=%async_computation | async-start | bytes 8192 | tf_op jit(solution)/shard_map/all_to_all | solution.py:90
  19.6 11.1 %collective-permute-start.1 = (bf16[16,768]{1,0:T(8,128)(2,1)S(1)}, bf16[16,768]{1,0:T(8,128)(2,1)S(1)}, u32[]{:S(2)}, u32[]{:S(2)}) collective-permute-start(bf16[16,768]{1,0:T(8,128)(2,1)S(1)} %get-tuple-element.12), channel_id=1, source_target_pairs={{1,0},{2,1},{3,2},{4,3},{5,4},{6,5},{7,6},{9,8},{10,9},{11,10},{12... | collective-permute-start | bytes 73736 | tf_op jit(solution)/shard_map/ppermute | solution.py:21
  23.0 6.6 %collective-permute-start = (bf16[16,768]{1,0:T(8,128)(2,1)S(1)}, bf16[16,768]{1,0:T(8,128)(2,1)S(1)}, u32[]{:S(2)}, u32[]{:S(2)}) collective-permute-start(bf16[16,768]{1,0:T(8,128)(2,1)S(1)} %get-tuple-element.13), channel_id=1, source_target_pairs={{0,1},{1,2},{2,3},{3,4},{4,5},{5,6},{6,7},{8,9},{9,10},{10,11},{11... | collective-permute-start | bytes 73736 | tf_op jit(solution)/shard_map/ppermute | solution.py:19
  30.8 12.3 %copy-start.6 = (bf16[768]{0:T(1024)(128)(2,1)S(1)}, bf16[768]{0:T(1024)(128)(2,1)}, u32[]{:S(2)}) copy-start(bf16[768]{0:T(1024)(128)(2,1)} %param.12) | copy-start | bytes 4612
  30.8 12.3 %copy-start.7 = (s32[1,128]{1,0:T(1,128)S(1)}, s32[1,128]{1,0:T(1,128)}, u32[]{:S(2)}) copy-start(s32[1,128]{1,0:T(1,128)} %param.15) | copy-start | bytes 1540
  35.9 15.1 %copy-start.8 = (f32[1,128]{1,0:T(1,128)S(1)}, f32[1,128]{1,0:T(1,128)}, u32[]{:S(2)}) copy-start(f32[1,128]{1,0:T(1,128)} %param.14) | copy-start | bytes 1540
  37.1 24.6 %copy-start.5 = (bf16[1,128,768]{2,1,0:T(8,128)(2,1)S(1)}, bf16[1,128,768]{2,1,0:T(8,128)(2,1)}, u32[]{:S(2)}) copy-start(bf16[1,128,768]{2,1,0:T(8,128)(2,1)} %param.13) | copy-start | bytes 589828
  37.9 12.2 %all-to-all-start.1 = ((bf16[8,32,768]{2,1,0:T(8,128)(2,1)}), bf16[8,32,768]{2,1,0:T(8,128)(2,1)S(1)}, u32[]{:S(2)}, u32[]{:S(2)}) async-start(bf16[8,32,768]{2,1,0:T(8,128)(2,1)} %broadcast_select_fusion), calls=%async_computation.1 | async-start | bytes 786432 | tf_op jit(solution)/shard_map/all_to_all | solution.py:92
  51.0 10.7 %copy-start.2 = (bf16[128,768]{1,0:T(8,128)(2,1)}, bf16[128,768]{1,0:T(8,128)(2,1)S(1)}, u32[]{:S(2)}) copy-start(bf16[128,768]{1,0:T(8,128)(2,1)S(1)} %gather_fusion.2) | copy-start | bytes 589828
  51.4 10.3 %copy-start.4 = (bf16[128,768]{1,0:T(8,128)(2,1)}, bf16[128,768]{1,0:T(8,128)(2,1)S(1)}, u32[]{:S(2)}) copy-start(bf16[128,768]{1,0:T(8,128)(2,1)S(1)} %fusion.13) | copy-start | bytes 589828
  53.8 14.4 %all-to-all-start.2 = ((bf16[8,32,768]{2,1,0:T(8,128)(2,1)}), bf16[8,32,768]{2,1,0:T(8,128)(2,1)}, u32[]{:S(2)}, u32[]{:S(2)}) async-start(bf16[8,32,768]{2,1,0:T(8,128)(2,1)} %bitcast.16), calls=%async_computation.2 | async-start | bytes 786432 | tf_op jit(solution)/shard_map/all_to_all | solution.py:115
  60.5 94.0 %reduce-scatter.7.cloned.1.call-start = ((), (), s32[]{:S(2)}) async-start(), calls=%async_computation.6 | async-start | bytes 8847360
  69.9 10.3 %copy-start.3 = (bf16[128,768]{1,0:T(8,128)(2,1)}, bf16[128,768]{1,0:T(8,128)(2,1)S(1)}, u32[]{:S(2)}) copy-start(bf16[128,768]{1,0:T(8,128)(2,1)S(1)} %fusion.1) | copy-start | bytes 589828
  90.3 164.5 %reduce-scatter.5.cloned.1.call-start = ((), (), s32[]{:S(2)}) async-start(), calls=%async_computation.5 | async-start | bytes 5308416 | tf_op jit(solution)/shard_map/reduce_scatter | solution.py:151
  159.7 14.8 %copy-start.1 = (bf16[1,128,768]{2,1,0:T(8,128)(2,1)S(1)}, bf16[1,128,768]{2,1,0:T(8,128)(2,1)}, u32[]{:S(2)}) copy-start(bf16[1,128,768]{2,1,0:T(8,128)(2,1)} %param.9) | copy-start | bytes 589828
  160.5 6.7 %collective-permute-start.2 = (bf16[16,768]{1,0:T(8,128)(2,1)S(1)}, bf16[16,768]{1,0:T(8,128)(2,1)S(1)}, u32[]{:S(2)}, u32[]{:S(2)}) collective-permute-start(bf16[16,768]{1,0:T(8,128)(2,1)S(1)} %get-tuple-element.10), channel_id=1, source_target_pairs={{0,1},{1,2},{2,3},{3,4},{4,5},{5,6},{6,7},{8,9},{9,10},{10,11},{11... | collective-permute-start | bytes 73736 | tf_op jit(solution)/shard_map/ppermute | solution.py:19
  163.9 5.7 %collective-permute-start.3 = (bf16[16,768]{1,0:T(8,128)(2,1)S(1)}, bf16[16,768]{1,0:T(8,128)(2,1)S(1)}, u32[]{:S(2)}, u32[]{:S(2)}) collective-permute-start(bf16[16,768]{1,0:T(8,128)(2,1)S(1)} %get-tuple-element.11), channel_id=1, source_target_pairs={{1,0},{2,1},{3,2},{4,3},{5,4},{6,5},{7,6},{9,8},{10,9},{11,10},{12... | collective-permute-start | bytes 73736 | tf_op jit(solution)/shard_map/ppermute | solution.py:21
Sparse Core Ops, SparseCore 0:
  90.5 63.9 reduce-scatter.6
  159.8 94.9 reduce-scatter.4
where the time goes:
time: 268 us; the launch traced here: 264 us
  waiting for transfers between devices  160 us (60%)
  starting transfers between devices  30.4 us (11%)
  local copies, waits for them, and re-layouts  21.1 us (8%)
  matrix products  19.3 us (7%)
  other arithmetic  18.6 us (7%)
  between operations  14.3 us (5%)
    reduce_scatter x1, waiting for transfers between devices, per_device(): lax.psum_scatter(column_share, 'seq', scatter_dimension=0, tiled=True)  79.3 us
    unnamed x3, waiting for transfers between devices  64.1 us
    unnamed x21, local copies, waits for them, and re-layouts  15 us
    dot_general x4, matrix products, contract_rows(): lax.dot_general(left_side, right_side, (((0,), (0,)), ((), ())), preferre...  8.42 us
    ppermute x2, starting transfers between devices, with_halo(): lax.ppermute(head, axis, [((i + 1) % count, i) for i in range(ends)])  6.72 us
    all_to_all x1, starting transfers between devices, per_device(): lax.all_to_all(outgoing, 'seq', split_axis=0, concat_axis=0, tiled=True)  6.65 us
    all_to_all x1, waiting for transfers between devices, per_device(): lax.all_to_all(picked, 'seq', split_axis=0, concat_axis=0, tiled=True)  6.13 us
    all_to_all x1, starting transfers between devices, per_device(): lax.all_to_all(request, 'seq', split_axis=0, concat_axis=0, tiled=True)  6.05 us
  transfers between devices with their start and end apart: 9, of which 6 were waited for; matrix products, arithmetic and copies ran while one was open for 6% of the time, Pallas kernels for 0%

commit v1 on v0

--- a/solution.py
+++ b/solution.py
@@ -138,17 +138,27 @@
     input_grad = norm_inverse * normed_grad - input_values * norm_inverse**3 * jnp.mean(
         normed_grad * input_values, axis=1, keepdims=True
     )
-    conv_term = contract_rows(columns, preact_grad) * (
+    tap_rows = tap_count * chan_count
+    chunk = (tap_rows + out_count) // shards
+    sources = jnp.concatenate([columns, pair_feature], axis=1)
+    sources = lax.all_to_all(sources, "seq", split_axis=1, concat_axis=0, tiled=True)
+    sources = lax.all_gather(sources, "dp", axis=0, tiled=True)
+    head_side = lax.all_to_all(head_delta, "dp", split_axis=1, concat_axis=0, tiled=True)
+    head_side = lax.all_gather(
+        head_side.reshape(-1, row_count, head_side.shape[1]), "seq", axis=1, tiled=True
+    )
+    conv_side = lax.all_to_all(preact_grad, "dp", split_axis=1, concat_axis=0, tiled=True)
+    conv_side = lax.all_gather(
+        conv_side.reshape(-1, row_count, conv_side.shape[1]), "seq", axis=1, tiled=True
+    )
+    conv_term = contract_rows(sources, conv_side.reshape(-1, conv_side.shape[2])) * (
         1.0 / math.sqrt(batch_total * row_count * shards)
     )
-    head_term = contract_rows(pair_feature, head_delta) * (
+    head_term = contract_rows(sources, head_side.reshape(-1, head_side.shape[2])) * (
         1.0 / math.sqrt(batch_total * pair_count * shards)
     )
-    grad_term = jnp.concatenate([conv_term, head_term], axis=0)
-    column_share = lax.psum_scatter(
-        grad_term.astype(jnp.bfloat16), "dp", scatter_dimension=1, tiled=True
-    ).astype(jnp.float32)
-    weight_grads = lax.psum_scatter(column_share, "seq", scatter_dimension=0, tiled=True)
+    row_of = lax.axis_index("seq") * chunk + jnp.arange(chunk, dtype=jnp.int32)
+    weight_grads = jnp.where((row_of < tap_rows)[:, None], conv_term, head_term)
     return (input_grad.astype(jnp.bfloat16)[None], weight_grads)
 
 

time: 268 us -> 218 us (0.81)
  waiting for transfers between devices: 160 us -> 65 us
  blocking collectives: 0 us -> 58.3 us
  local copies, waits for them, and re-layouts: 21.1 us -> 13 us
  other arithmetic: 18.6 us -> 13.6 us
    reduce_scatter x1 -> x0, waiting for transfers between devices: 79.3 us -> none  [per_device(): lax.psum_scatter(column_share, 'seq', scatter_dimension=0, tiled=True)]
    unnamed x3, waiting for transfers between devices: 64.1 us -> 0.05 us
    all_to_all x0 -> x3, blocking collectives: none -> 58.3 us  [the longest x1 40.9 us: per_device(): lax.all_to_all(sources, 'seq', split_axis=1, concat_axis=0, tiled=True)]
    all_gather x0 -> x3, waiting for transfers between devices: none -> 44.2 us  [the longest x1 35.4 us: per_device(): sources = lax.all_gather(sources, 'dp', axis=0, tiled=True)]
    unnamed x21 -> x16, local copies, waits for them, and re-layouts: 15 us -> 0.04 us
    all_to_all x1, waiting for transfers between devices: 4.01 us -> 11.6 us  [per_device(): lax.all_to_all(outgoing, 'seq', split_axis=0, concat_axis=0, tiled=True)]
    concatenate x2 -> x1, other arithmetic: 6.06 us -> 0.76 us  [per_device(): sources = jnp.concatenate([columns, pair_feature], axis=1)]
    reshape x0 -> x2, local copies, waits for them, and re-layouts: none -> 4.35 us  [the longest x1 2.78 us: per_device(): conv_side.reshape(-1, conv_side.shape[2])]
  transfers between devices with their start and end apart: 9 -> 10, of which waited for: 6 -> 5; matrix products, arithmetic and copies ran while one was open for 6% -> 12% of each run, Pallas kernels for 0% -> 0%
where the time goes in v1:
time: 218 us; the launch traced here: 215 us
  waiting for transfers between devices  65 us (30%)
  blocking collectives  58.3 us (27%)
  starting transfers between devices  31.1 us (14%)
  matrix products  19.7 us (9%)
  between operations  14 us (6%)
  other arithmetic  13.6 us (6%)
  local copies, waits for them, and re-layouts  13 us (6%)
    all_to_all x1, blocking collectives, per_device(): lax.all_to_all(sources, 'seq', split_axis=1, concat_axis=0, tiled=True)  40.9 us
    all_gather x1, waiting for transfers between devices, per_device(): sources = lax.all_gather(sources, 'dp', axis=0, tiled=True)  35.4 us
    all_to_all x1, waiting for transfers between devices, per_device(): lax.all_to_all(outgoing, 'seq', split_axis=0, concat_axis=0, tiled=True)  11.6 us
    all_to_all x1, blocking collectives, per_device(): lax.all_to_all(preact_grad, 'dp', split_axis=1, concat_axis=0, tiled=True)  10.2 us
    dot_general x4, matrix products, contract_rows(): lax.dot_general(left_side, right_side, (((0,), (0,)), ((), ())), preferre...  8.81 us
    all_gather x1, waiting for transfers between devices, per_device(): lax.all_gather(conv_side.reshape(-1, row_count, conv_side.shape[1]), 'seq...  8.75 us
    all_to_all x1, blocking collectives, per_device(): lax.all_to_all(head_delta, 'dp', split_axis=1, concat_axis=0, tiled=True)  7.26 us
    ppermute x2, starting transfers between devices, with_halo(): lax.ppermute(tail, axis, [(i, (i + 1) % count) for i in range(ends)])  6.88 us
  transfers between devices with their start and end apart: 10, of which 5 were waited for; matrix products, arithmetic and copies ran while one was open for 12% of the time, Pallas kernels for 0%

profile of v1, /device:TPU:26, one launch (start us, length us, event | category | flops | bytes accessed | tf_op | source)
XLA Modules:
  0.0 214.8 jit_solution(10204450921731705878)
XLA Ops:
  7.2 0.9 fusion.55
  8.2 0.8 select_reduce_fusion
  9.1 0.7 fusion.58
  9.7 1.1 scatter_custom_fusion
  10.8 0.7 all_to_all.50
  11.5 6.1 %all-to-all-start = ((s32[8,1,32]{2,1,0:T(1,128)}), s32[8,1,32]{2,1,0:T(1,128)S(1)}, u32[]{:S(2)}, u32[]{:S(2)}) async-start(s32[8,1,32]{2,1,0:T(1,128)} %all_to_all.50), calls=%async_computation | async-start | bytes 8192 | tf_op jit(solution)/shard_map/all_to_all | solution.py:90
  17.6 1.0 fusion.19
  18.6 1.0 fusion.20
  19.7 3.4 %collective-permute-start = (bf16[16,768]{1,0:T(8,128)(2,1)S(1)}, bf16[16,768]{1,0:T(8,128)(2,1)S(1)}, u32[]{:S(2)}, u32[]{:S(2)}) collective-permute-start(bf16[16,768]{1,0:T(8,128)(2,1)S(1)} %get-tuple-element.17), channel_id=1, source_target_pairs={{0,1},{1,2},{2,3},{3,4},{4,5},{5,6},{6,7},{8,9},{9,10},{10,11},{11... | collective-permute-start | bytes 73736 | tf_op jit(solution)/shard_map/ppermute | solution.py:19
  23.1 3.4 %collective-permute-start.1 = (bf16[16,768]{1,0:T(8,128)(2,1)S(1)}, bf16[16,768]{1,0:T(8,128)(2,1)S(1)}, u32[]{:S(2)}, u32[]{:S(2)}) collective-permute-start(bf16[16,768]{1,0:T(8,128)(2,1)S(1)} %get-tuple-element.16), channel_id=1, source_target_pairs={{1,0},{2,1},{3,2},{4,3},{5,4},{6,5},{7,6},{9,8},{10,9},{11,10},{12... | collective-permute-start | bytes 73736 | tf_op jit(solution)/shard_map/ppermute | solution.py:21
  26.6 0.7 constant_dynamic-update-slice_fusion.5
  27.3 0.7 fusion.46
  28.0 0.8 constant_dynamic-update-slice_fusion.4
  28.9 0.7 constant_dynamic-update-slice_fusion.3
  29.6 0.7 fusion.48
  30.3 5.1 %fusion.8 = (bf16[128,768]{1,0:T(8,128)(2,1)S(1)}, f32[128,768]{1,0:T(8,128)}) fusion(bf16[128,3840]{1,0:T(8,128)(2,1)S(1)} %get-tuple-element.5, bf16[3840,768]{1,0:T(8,128)(2,1)} %param.10), kind=kOutput, calls=%fused_computation.28 | convolution fusion | flops 761364480 | bytes 7471104 | tf_op jit(solution)/shard_map/dot_general | solution.py:75
  35.4 1.2 gather_fusion.1
  36.6 0.9 broadcast_select_fusion
  37.5 5.9 %all-to-all-start.1 = ((bf16[8,32,768]{2,1,0:T(8,128)(2,1)}), bf16[8,32,768]{2,1,0:T(8,128)(2,1)S(1)}, u32[]{:S(2)}, u32[]{:S(2)}) async-start(bf16[8,32,768]{2,1,0:T(8,128)(2,1)} %broadcast_select_fusion), calls=%async_computation.1 | async-start | bytes 786432 | tf_op jit(solution)/shard_map/all_to_all | solution.py:92
  43.5 0.9 gather_fusion
  44.3 6.1 %all-to-all-done.1 = bf16[8,32,768]{2,1,0:T(8,128)(2,1)S(1)} async-done(((bf16[8,32,768]{2,1,0:T(8,128)(2,1)}), bf16[8,32,768]{2,1,0:T(8,128)(2,1)S(1)}, u32[]{:S(2)}, u32[]{:S(2)}) %all-to-all-start.1) | async-done | bytes 393248 | tf_op jit(solution)/shard_map/all_to_all | solution.py:92
  50.5 0.9 gather_fusion.2
  51.4 0.4 fusion.14
  51.9 7.3 %all_to_all.70 = bf16[128,4,192]{0,2,1:T(8,128)(2,1)} all-to-all(bf16[128,4,192]{0,2,1:T(8,128)(2,1)S(1)} %bitcast.73), channel_id=1, replica_groups=mesh['dp'=4,'seq'=8] {'dp'}, dimensions={1} | all-to-all | bytes 393216 | tf_op jit(solution)/shard_map/all_to_all | solution.py:146
  59.2 0.5 fusion.64
  59.8 1.9 scatter_custom_fusion.1
  61.7 6.3 %all-to-all-start.2 = ((bf16[8,32,768]{2,1,0:T(8,128)(2,1)}), bf16[8,32,768]{2,1,0:T(8,128)(2,1)S(1)}, u32[]{:S(2)}, u32[]{:S(2)}) async-start(bf16[8,32,768]{2,1,0:T(8,128)(2,1)} %bitcast.16), calls=%async_computation.2 | async-start | bytes 786432 | tf_op jit(solution)/shard_map/all_to_all | solution.py:115
  68.0 0.5 broadcast.170
  68.5 0.7 reduce.3
  69.2 0.3 convolution_add_fusion.1
  69.6 11.6 %all-to-all-done.2 = bf16[8,32,768]{2,1,0:T(8,128)(2,1)S(1)} async-done(((bf16[8,32,768]{2,1,0:T(8,128)(2,1)}), bf16[8,32,768]{2,1,0:T(8,128)(2,1)S(1)}, u32[]{:S(2)}, u32[]{:S(2)}) %all-to-all-start.2) | async-done | bytes 393248 | tf_op jit(solution)/shard_map/all_to_all | solution.py:115
  81.2 1.4 fusion.2
  82.7 10.2 %all_to_all.71 = bf16[128,4,192]{0,2,1:T(8,128)(2,1)} all-to-all(bf16[128,4,192]{0,2,1:T(8,128)(2,1)S(1)} %bitcast.74), channel_id=1, replica_groups=mesh['dp'=4,'seq'=8] {'dp'}, dimensions={1} | all-to-all | bytes 393216 | tf_op jit(solution)/shard_map/all_to_all | solution.py:150
  93.0 0.8 fusion.49
  93.7 1.7 copy.24
  95.4 40.9 %all_to_all.72 = bf16[128,8,576]{0,2,1:T(8,128)(2,1)S(1)} all-to-all(bf16[128,8,576]{0,2,1:T(8,128)(2,1)S(1)} %bitcast.65), channel_id=1, replica_groups=mesh['dp'=4,'seq'=8] {'seq'}, dimensions={1} | all-to-all | bytes 2359296 | tf_op jit(solution)/shard_map/all_to_all | solution.py:144
  136.3 1.3 copy_bitcast_fusion
  137.6 2.5 %collective-permute-start.3 = (bf16[16,768]{1,0:T(8,128)(2,1)S(1)}, bf16[16,768]{1,0:T(8,128)(2,1)S(1)}, u32[]{:S(2)}, u32[]{:S(2)}) collective-permute-start(bf16[16,768]{1,0:T(8,128)(2,1)S(1)} %get-tuple-element.15), channel_id=1, source_target_pairs={{1,0},{2,1},{3,2},{4,3},{5,4},{6,5},{7,6},{9,8},{10,9},{11,10},{12... | collective-permute-start | bytes 73736 | tf_op jit(solution)/shard_map/ppermute | solution.py:21
  140.1 3.5 %collective-permute-start.2 = (bf16[16,768]{1,0:T(8,128)(2,1)S(1)}, bf16[16,768]{1,0:T(8,128)(2,1)S(1)}, u32[]{:S(2)}, u32[]{:S(2)}) collective-permute-start(bf16[16,768]{1,0:T(8,128)(2,1)S(1)} %get-tuple-element.14), channel_id=1, source_target_pairs={{0,1},{1,2},{2,3},{3,4},{4,5},{5,6},{6,7},{8,9},{9,10},{10,11},{11... | collective-permute-start | bytes 73736 | tf_op jit(solution)/shard_map/ppermute | solution.py:19
  143.7 3.1 %collective-permute-done.2 = bf16[16,768]{1,0:T(8,128)(2,1)S(1)} collective-permute-done((bf16[16,768]{1,0:T(8,128)(2,1)S(1)}, bf16[16,768]{1,0:T(8,128)(2,1)S(1)}, u32[]{:S(2)}, u32[]{:S(2)}) %collective-permute-start.2) | collective-permute-done | bytes 24608 | tf_op jit(solution)/shard_map/ppermute | solution.py:19
  146.7 4.8 %fusion.32 = f32[160,3840]{1,0:T(8,128)S(1)} fusion(bf16[3840,768]{1,0:T(8,128)(2,1)} %param.10, bf16[16,768]{1,0:T(8,128)(2,1)S(1)} %collective-permute-done.3, bf16[128,768]{1,0:T(8,128)(2,1)S(1)} %fusion.2, bf16[16,768]{1,0:T(8,128)(2,1)S(1)} %collective-permute-done.2), kind=kOutput, calls=%fused_computation.65 | convolution fusion | flops 944455680 | bytes 8601600 | tf_op jit(solution)/shard_map/dot_general | solution.py:125
  151.8 0.8 fusion.40
  152.6 1.6 copy.32
  154.2 8.8 %all-gather.6.cloned.1.call-done = bf16[4,1024,192]{1,2,0:T(8,128)(2,1)} async-done(((bf16[4,128,192]{1,2,0:T(8,128)(2,1)}), bf16[4,1024,192]{1,2,0:T(8,128)(2,1)}) %all-gather.6.cloned.1.call-update) | async-done | bytes 1572880 | tf_op jit(solution)/shard_map/all_gather | solution.py:151
  162.9 2.8 %copy.31 = bf16[4,24,8,1024]{3,2,0,1:T(8,128)(2,1)} copy(bf16[4,24,8,1024]{3,2,1,0:T(8,128)(2,1)} %bitcast.67) | data formatting | bytes 3145728 | tf_op jit(solution)/shard_map/reshape | solution.py:154
  165.7 35.4 %all-gather.4.cloned.1.call-done = bf16[4096,576]{0,1:T(8,128)(2,1)} async-done(((bf16[1024,576]{0,1:T(8,128)(2,1)}), bf16[4096,576]{0,1:T(8,128)(2,1)}) %all-gather.4.cloned.1.call-update) | async-done | bytes 4718608 | tf_op jit(solution)/shard_map/all_gather | solution.py:145
  201.1 4.4 %convolution_multiply_fusion = f32[576,192]{0,1:T(8,128)S(1)} fusion(bf16[4096,576]{0,1:T(8,128)(2,1)} %all-gather.4.cloned.1.call-done, bf16[4096,192]{0,1:T(8,128)(2,1)S(1)} %bitcast.68), kind=kOutput, calls=%fused_computation.5 | convolution fusion | flops 906080256 | bytes 6733824 | tf_op jit(solution)/shard_map/dot_general | solution.py:35
  205.6 2.7 %fusion.1 = f32[576,192]{0,1:T(8,128)} fusion(f32[576,192]{0,1:T(8,128)S(1)} %convolution_multiply_fusion, bf16[4096,576]{0,1:T(8,128)(2,1)S(1)} %copy-done.6, bf16[4096,192]{0,1:T(8,128)(2,1)S(1)} %bitcast.69, pred[576]{0:T(1024)(128)(4,1)S(1)} %add_compare_fusion), kind=kOutput, calls=%fused_computation.10 | convolution fusion | flops 906190848 | bytes 7176768 | tf_op jit(solution)/shard_map/dot_general | solution.py:35
  (45 shorter events, 1.1 us)
Async XLA Ops:
  7.2 44.2 %copy-start = (bf16[768,768]{1,0:T(8,128)(2,1)S(1)}, bf16[768,768]{1,0:T(8,128)(2,1)}, u32[]{:S(2)}) copy-start(bf16[768,768]{1,0:T(8,128)(2,1)} %param.11) | copy-start | bytes 3538948
  7.2 20.8 %copy-start.1 = (bf16[1,128,768]{2,1,0:T(8,128)(2,1)S(1)}, bf16[1,128,768]{2,1,0:T(8,128)(2,1)}, u32[]{:S(2)}) copy-start(bf16[1,128,768]{2,1,0:T(8,128)(2,1)} %param.9) | copy-start | bytes 589828
  11.5 14.9 %all-to-all-start = ((s32[8,1,32]{2,1,0:T(1,128)}), s32[8,1,32]{2,1,0:T(1,128)S(1)}, u32[]{:S(2)}, u32[]{:S(2)}) async-start(s32[8,1,32]{2,1,0:T(1,128)} %all_to_all.50), calls=%async_computation | async-start | bytes 8192 | tf_op jit(solution)/shard_map/all_to_all | solution.py:90
  19.7 6.9 %collective-permute-start = (bf16[16,768]{1,0:T(8,128)(2,1)S(1)}, bf16[16,768]{1,0:T(8,128)(2,1)S(1)}, u32[]{:S(2)}, u32[]{:S(2)}) collective-permute-start(bf16[16,768]{1,0:T(8,128)(2,1)S(1)} %get-tuple-element.17), channel_id=1, source_target_pairs={{0,1},{1,2},{2,3},{3,4},{4,5},{5,6},{6,7},{8,9},{9,10},{10,11},{11... | collective-permute-start | bytes 73736 | tf_op jit(solution)/shard_map/ppermute | solution.py:19
  23.1 5.8 %collective-permute-start.1 = (bf16[16,768]{1,0:T(8,128)(2,1)S(1)}, bf16[16,768]{1,0:T(8,128)(2,1)S(1)}, u32[]{:S(2)}, u32[]{:S(2)}) collective-permute-start(bf16[16,768]{1,0:T(8,128)(2,1)S(1)} %get-tuple-element.16), channel_id=1, source_target_pairs={{1,0},{2,1},{3,2},{4,3},{5,4},{6,5},{7,6},{9,8},{10,9},{11,10},{12... | collective-permute-start | bytes 73736 | tf_op jit(solution)/shard_map/ppermute | solution.py:21
  36.6 6.8 %copy-start.4 = (bf16[768]{0:T(1024)(128)(2,1)S(1)}, bf16[768]{0:T(1024)(128)(2,1)}, u32[]{:S(2)}) copy-start(bf16[768]{0:T(1024)(128)(2,1)} %param.12) | copy-start | bytes 4612
  36.6 6.8 %copy-start.5 = (s32[1,128]{1,0:T(1,128)S(1)}, s32[1,128]{1,0:T(1,128)}, u32[]{:S(2)}) copy-start(s32[1,128]{1,0:T(1,128)} %param.15) | copy-start | bytes 1540
  37.5 13.0 %all-to-all-start.1 = ((bf16[8,32,768]{2,1,0:T(8,128)(2,1)}), bf16[8,32,768]{2,1,0:T(8,128)(2,1)S(1)}, u32[]{:S(2)}, u32[]{:S(2)}) async-start(bf16[8,32,768]{2,1,0:T(8,128)(2,1)} %broadcast_select_fusion), calls=%async_computation.1 | async-start | bytes 786432 | tf_op jit(solution)/shard_map/all_to_all | solution.py:92
  43.4 109.2 %all-gather.8.cloned.1.call-start = ((), (), s32[]{:S(2)}) async-start(), calls=%async_computation.8 | async-start | bytes 1769472 | tf_op jit(solution)/shard_map/all_gather | solution.py:147
  44.3 7.0 %copy-start.7 = (f32[1,128]{1,0:T(1,128)S(1)}, f32[1,128]{1,0:T(1,128)}, u32[]{:S(2)}) copy-start(f32[1,128]{1,0:T(1,128)} %param.14) | copy-start | bytes 1540
  59.8 9.5 %copy-start.3 = (bf16[1,128,768]{2,1,0:T(8,128)(2,1)S(1)}, bf16[1,128,768]{2,1,0:T(8,128)(2,1)}, u32[]{:S(2)}) copy-start(bf16[1,128,768]{2,1,0:T(8,128)(2,1)} %param.13) | copy-start | bytes 589828
  61.7 19.5 %all-to-all-start.2 = ((bf16[8,32,768]{2,1,0:T(8,128)(2,1)}), bf16[8,32,768]{2,1,0:T(8,128)(2,1)S(1)}, u32[]{:S(2)}, u32[]{:S(2)}) async-start(bf16[8,32,768]{2,1,0:T(8,128)(2,1)} %bitcast.16), calls=%async_computation.2 | async-start | bytes 786432 | tf_op jit(solution)/shard_map/all_to_all | solution.py:115
  68.0 94.9 %all-gather.6.cloned.1.call-start = ((), (), s32[]{:S(2)}) async-start(), calls=%async_computation.7 | async-start | bytes 1769472 | tf_op jit(solution)/shard_map/all_gather | solution.py:151
  92.9 108.2 %all-gather.4.cloned.1.call-start = ((), (), s32[]{:S(2)}) async-start(), calls=%async_computation.6 | async-start | bytes 5898240 | tf_op jit(solution)/shard_map/all_gather | solution.py:145
  137.6 6.1 %collective-permute-start.3 = (bf16[16,768]{1,0:T(8,128)(2,1)S(1)}, bf16[16,768]{1,0:T(8,128)(2,1)S(1)}, u32[]{:S(2)}, u32[]{:S(2)}) collective-permute-start(bf16[16,768]{1,0:T(8,128)(2,1)S(1)} %get-tuple-element.15), channel_id=1, source_target_pairs={{1,0},{2,1},{3,2},{4,3},{5,4},{6,5},{7,6},{9,8},{10,9},{11,10},{12... | collective-permute-start | bytes 73736 | tf_op jit(solution)/shard_map/ppermute | solution.py:21
  140.1 6.6 %collective-permute-start.2 = (bf16[16,768]{1,0:T(8,128)(2,1)S(1)}, bf16[16,768]{1,0:T(8,128)(2,1)S(1)}, u32[]{:S(2)}, u32[]{:S(2)}) collective-permute-start(bf16[16,768]{1,0:T(8,128)(2,1)S(1)} %get-tuple-element.14), channel_id=1, source_target_pairs={{0,1},{1,2},{2,3},{3,4},{4,5},{5,6},{6,7},{8,9},{9,10},{10,11},{11... | collective-permute-start | bytes 73736 | tf_op jit(solution)/shard_map/ppermute | solution.py:19
  201.1 4.4 %copy-start.2 = (bf16[4,24,8,1024]{3,2,0,1:T(8,128)(2,1)S(1)}, bf16[4,24,8,1024]{3,2,0,1:T(8,128)(2,1)}, u32[]{:S(2)}) copy-start(bf16[4,24,8,1024]{3,2,0,1:T(8,128)(2,1)} %copy.31) | copy-start | bytes 4718596
  201.1 4.5 %copy-start.6 = (bf16[4096,576]{0,1:T(8,128)(2,1)S(1)}, bf16[4096,576]{0,1:T(8,128)(2,1)}, u32[]{:S(2)}) copy-start(bf16[4096,576]{0,1:T(8,128)(2,1)} %all-gather.4.cloned.1.call-done) | copy-start | bytes 14155780
Sparse Core Ops, SparseCore 0:
  59.3 57.0 all-gather.7
  118.5 44.4 all-gather.5
  164.5 36.5 all-gather.3

commit v2 on v0

--- a/solution.py
+++ b/solution.py
@@ -64,7 +64,9 @@
     input_values = activations[0].astype(jnp.float32)
     norm_inverse = lax.rsqrt(jnp.mean(input_values * input_values, axis=1, keepdims=True) + 1e-05)
     normed = (input_values * norm_inverse).astype(jnp.bfloat16)
+    normed_all = lax.all_gather(normed, "seq", axis=0, tiled=True)
     padded = widened(normed, reach_rows)
+    tap_rows = tap_count * chan_count
     columns = jnp.concatenate(
         [
             padded[tap_index * DILATION : tap_index * DILATION + row_count]
@@ -138,17 +140,61 @@
     input_grad = norm_inverse * normed_grad - input_values * norm_inverse**3 * jnp.mean(
         normed_grad * input_values, axis=1, keepdims=True
     )
-    conv_term = contract_rows(columns, preact_grad) * (
+    chunk = (tap_rows + out_count) // shards
+    first = lax.axis_index("seq") * chunk
+    tap_low = jnp.minimum(first // chan_count, tap_count - 1)
+    tap_high = jnp.minimum(tap_low + 1, tap_count - 1)
+    all_rows = row_count * shards
+    gathered = jnp.pad(normed_all, ((reach_rows, reach_rows), (0, 0)))
+    pair_of_taps = jnp.concatenate(
+        [
+            lax.dynamic_slice_in_dim(gathered, tap_low * DILATION, all_rows, axis=0),
+            lax.dynamic_slice_in_dim(gathered, tap_high * DILATION, all_rows, axis=0),
+        ],
+        axis=1,
+    )
+    sources = lax.dynamic_slice_in_dim(pair_of_taps, first % chan_count, chunk, axis=1)
+    grad_all = lax.all_gather(preact_grad, "seq", axis=0, tiled=True)
+    conv_term = contract_rows(sources, grad_all) * (
         1.0 / math.sqrt(batch_total * row_count * shards)
     )
+    parts = lax.all_to_all(
+        conv_term.astype(jnp.bfloat16), "dp", split_axis=1, concat_axis=0, tiled=True
+    ).reshape(-1, chunk, out_count // lax.axis_size("dp"))
+    conv_share = jnp.sum(parts.astype(jnp.float32), axis=0)
     head_term = contract_rows(pair_feature, head_delta) * (
         1.0 / math.sqrt(batch_total * pair_count * shards)
     )
-    grad_term = jnp.concatenate([conv_term, head_term], axis=0)
-    column_share = lax.psum_scatter(
-        grad_term.astype(jnp.bfloat16), "dp", scatter_dimension=1, tiled=True
-    ).astype(jnp.float32)
-    weight_grads = lax.psum_scatter(column_share, "seq", scatter_dimension=0, tiled=True)
+    head_cells = lax.all_to_all(
+        head_term.astype(jnp.bfloat16), "dp", split_axis=1, concat_axis=0, tiled=True
+    ).reshape(-1, out_count, out_count // lax.axis_size("dp"))
+    head_share = jnp.sum(head_cells.astype(jnp.float32), axis=0)
+    head_parts = lax.all_to_all(
+        head_share.astype(jnp.bfloat16), "seq", split_axis=0, concat_axis=0, tiled=True
+    )
+    block = out_count // shards
+    head_block = jnp.sum(
+        head_parts.reshape(shards, block, -1).astype(jnp.float32), axis=0
+    )
+    per_owner = tap_count * chan_count // out_count + 1
+    skipped = tap_rows // block
+    head_rows = jnp.concatenate(
+        [
+            lax.ppermute(
+                head_block,
+                "seq",
+                [
+                    (i, (skipped + i) // per_owner)
+                    for i in range(shards)
+                    if (skipped + i) % per_owner == place
+                ],
+            )
+            for place in range(per_owner)
+        ],
+        axis=0,
+    )
+    row_of = first + jnp.arange(chunk, dtype=jnp.int32)
+    weight_grads = jnp.where((row_of < tap_rows)[:, None], conv_share, head_rows)
     return (input_grad.astype(jnp.bfloat16)[None], weight_grads)
 
 

time: 268 us -> 165 us (0.62); the launches traced: 264 us -> 164 us
  waiting for transfers between devices: 160 us -> 43.5 us
  starting transfers between devices: 30.4 us -> 57.2 us
  local copies, waits for them, and re-layouts: 21.1 us -> 13.4 us
  other arithmetic: 18.6 us -> 14.6 us
    reduce_scatter x1 -> x0, waiting for transfers between devices: 79.3 us -> none  [per_device(): lax.psum_scatter(column_share, 'seq', scatter_dimension=0, tiled=True)]
    unnamed x3 -> x2, waiting for transfers between devices: 64.1 us -> 0.03 us
    all_gather x0 -> x2, waiting for transfers between devices: none -> 17.3 us  [the longest x1 17.3 us: per_device(): grad_all = lax.all_gather(preact_grad, 'seq', axis=0, tiled=True)]
    unnamed x21 -> x16, local copies, waits for them, and re-layouts: 15 us -> 0.05 us
    all_to_all x0 -> x3, starting transfers between devices: none -> 14.8 us  [the longest x1 6.8 us: per_device(): lax.all_to_all(head_share.astype(jnp.bfloat16), 'seq', split_axis=0, conc...]
    ppermute x0 -> x6, starting transfers between devices: none -> 10.2 us  [per_device(): lax.ppermute(head_block, 'seq', [(i, (skipped + i) // per_owner) for i in...]
    ppermute x0 -> x6, waiting for transfers between devices: none -> 7.07 us  [per_device(): lax.ppermute(head_block, 'seq', [(i, (skipped + i) // per_owner) for i in...]
    concatenate x1 -> x0, other arithmetic: 6.05 us -> none  [per_device(): grad_term = jnp.concatenate([conv_term, head_term], axis=0)]
  transfers between devices with their start and end apart: 9 -> 18, of which waited for: 6 -> 8; matrix products, arithmetic and copies ran while one was open for 6% -> 26% of each run, Pallas kernels for 0% -> 0%
where the time goes in v2:
time: 165 us; the launch traced here: 164 us
  starting transfers between devices  57.2 us (35%)
  waiting for transfers between devices  43.5 us (26%)
  matrix products  20.8 us (13%)
  other arithmetic  14.6 us (9%)
  between operations  14.4 us (9%)
  local copies, waits for them, and re-layouts  13.4 us (8%)
    all_gather x1, waiting for transfers between devices, per_device(): grad_all = lax.all_gather(preact_grad, 'seq', axis=0, tiled=True)  17.3 us
    all_to_all x1, waiting for transfers between devices, per_device(): lax.all_to_all(picked, 'seq', split_axis=0, concat_axis=0, tiled=True)  11.9 us
    ppermute x6, starting transfers between devices, per_device(): lax.ppermute(head_block, 'seq', [(i, (skipped + i) // per_owner) for i in...  10.2 us
    dot_general x4, matrix products, contract_rows(): lax.dot_general(left_side, right_side, (((0,), (0,)), ((), ())), preferre...  8.57 us
    ppermute x6, waiting for transfers between devices, per_device(): lax.ppermute(head_block, 'seq', [(i, (skipped + i) // per_owner) for i in...  7.07 us
    ppermute x2, starting transfers between devices, with_halo(): lax.ppermute(head, axis, [((i + 1) % count, i) for i in range(ends)])  7.06 us
    all_to_all x1, starting transfers between devices, per_device(): lax.all_to_all(head_share.astype(jnp.bfloat16), 'seq', split_axis=0, conc...  6.8 us
    all_to_all x1, starting transfers between devices, per_device(): lax.all_to_all(outgoing, 'seq', split_axis=0, concat_axis=0, tiled=True)  6.76 us
  transfers between devices with their start and end apart: 18, of which 8 were waited for; matrix products, arithmetic and copies ran while one was open for 26% of the time, Pallas kernels for 0%

profile of v2, /device:TPU:26, one launch (start us, length us, event | category | flops | bytes accessed | tf_op | source)
XLA Modules:
  0.0 163.9 jit_solution(13264200625433239200)
XLA Ops:
  7.2 0.9 fusion.56
  8.2 0.8 select_reduce_fusion
  9.1 0.7 fusion.60
  9.7 1.1 scatter_custom_fusion
  10.8 0.7 all_to_all.38
  11.5 6.1 %all-to-all-start = ((s32[8,1,32]{2,1,0:T(1,128)}), s32[8,1,32]{2,1,0:T(1,128)S(1)}, u32[]{:S(2)}, u32[]{:S(2)}) async-start(s32[8,1,32]{2,1,0:T(1,128)} %all_to_all.38), calls=%async_computation | async-start | bytes 8192 | tf_op jit(solution)/shard_map/all_to_all | solution.py:92
  17.6 1.0 fusion.20
  18.6 1.7 %fusion.21 = bf16[128,768]{1,0:T(8,128)(2,1)} fusion(bf16[1,128,768]{2,1,0:T(8,128)(2,1)} %param.9, f32[128]{0:T(128)S(1)} %get-tuple-element.11), kind=kLoop, calls=%fused_computation.45 | loop fusion | flops 294912 | bytes 393728 | tf_op jit(solution)/shard_map/convert_element_type | solution.py:66
  20.4 0.8 fusion.66
  21.2 3.4 %collective-permute-start = (bf16[16,768]{1,0:T(8,128)(2,1)S(1)}, bf16[16,768]{1,0:T(8,128)(2,1)S(1)}, u32[]{:S(2)}, u32[]{:S(2)}) collective-permute-start(bf16[16,768]{1,0:T(8,128)(2,1)S(1)} %get-tuple-element.9), channel_id=1, source_target_pairs={{0,1},{1,2},{2,3},{3,4},{4,5},{5,6},{6,7},{8,9},{9,10},{10,11},{11... | collective-permute-start | bytes 73736 | tf_op jit(solution)/shard_map/ppermute | solution.py:19
  24.5 3.4 %collective-permute-start.1 = (bf16[16,768]{1,0:T(8,128)(2,1)S(1)}, bf16[16,768]{1,0:T(8,128)(2,1)S(1)}, u32[]{:S(2)}, u32[]{:S(2)}) collective-permute-start(bf16[16,768]{1,0:T(8,128)(2,1)S(1)} %get-tuple-element.8), channel_id=1, source_target_pairs={{1,0},{2,1},{3,2},{4,3},{5,4},{6,5},{7,6},{9,8},{10,9},{11,10},{12... | collective-permute-start | bytes 73736 | tf_op jit(solution)/shard_map/ppermute | solution.py:21
  28.0 0.9 fusion.42
  29.0 0.9 fusion.48
  30.3 5.1 %fusion.9 = (bf16[128,768]{1,0:T(8,128)(2,1)S(1)}, f32[128,768]{1,0:T(8,128)}) fusion(bf16[128,3840]{1,0:T(8,128)(2,1)S(1)} %fusion.47, bf16[3840,768]{1,0:T(8,128)(2,1)} %param.10), kind=kOutput, calls=%fused_computation.33 | convolution fusion | flops 761364480 | bytes 7471104 | tf_op jit(solution)/shard_map/dot_general | solution.py:77
  35.4 1.2 gather_fusion.1
  36.7 0.9 broadcast_select_fusion
  37.5 5.9 %all-to-all-start.1 = ((bf16[8,32,768]{2,1,0:T(8,128)(2,1)}), bf16[8,32,768]{2,1,0:T(8,128)(2,1)S(1)}, u32[]{:S(2)}, u32[]{:S(2)}) async-start(bf16[8,32,768]{2,1,0:T(8,128)(2,1)} %broadcast_select_fusion), calls=%async_computation.1 | async-start | bytes 786432 | tf_op jit(solution)/shard_map/all_to_all | solution.py:94
  43.5 0.9 gather_fusion
  44.4 11.9 %all-to-all-done.1 = bf16[8,32,768]{2,1,0:T(8,128)(2,1)S(1)} async-done(((bf16[8,32,768]{2,1,0:T(8,128)(2,1)}), bf16[8,32,768]{2,1,0:T(8,128)(2,1)S(1)}, u32[]{:S(2)}, u32[]{:S(2)}) %all-to-all-start.1) | async-done | bytes 393248 | tf_op jit(solution)/shard_map/all_to_all | solution.py:94
  56.2 0.9 gather_fusion.2
  58.1 1.9 %scatter_custom_fusion.1 = bf16[256,768]{1,0:T(8,128)(2,1)} fusion(s32[128]{0:T(128)S(1)} %fusion.60, f32[128,768]{1,0:T(8,128)S(1)} %fusion.67, bf16[128,768]{1,0:T(8,128)(2,1)S(1)} %gather_fusion, bf16[]{:T(256)} %constant.132.clone.1), kind=kCustom, calls=%fused_computation.86 | custom fusion | flops 294912 | bytes 983042 | tf_op jit(solution)/shard_map/scatter | solution.py:114
  60.0 6.8 %all-to-all-start.2 = ((bf16[8,32,768]{2,1,0:T(8,128)(2,1)}), bf16[8,32,768]{2,1,0:T(8,128)(2,1)S(1)}, u32[]{:S(2)}, u32[]{:S(2)}) async-start(bf16[8,32,768]{2,1,0:T(8,128)(2,1)} %bitcast.16), calls=%async_computation.2 | async-start | bytes 786432 | tf_op jit(solution)/shard_map/all_to_all | solution.py:117
  67.3 0.7 reduce.7
  68.4 5.1 %all-to-all-done.2 = bf16[8,32,768]{2,1,0:T(8,128)(2,1)S(1)} async-done(((bf16[8,32,768]{2,1,0:T(8,128)(2,1)}), bf16[8,32,768]{2,1,0:T(8,128)(2,1)S(1)}, u32[]{:S(2)}, u32[]{:S(2)}) %all-to-all-start.2) | async-done | bytes 393248 | tf_op jit(solution)/shard_map/all_to_all | solution.py:117
  73.5 2.1 %fusion.3 = bf16[128,768]{1,0:T(8,128)(2,1)} fusion(f32[128,768]{1,0:T(8,128)S(1)} %convolution_add_fusion.1, bf16[256,768]{1,0:T(8,128)(2,1)S(1)} %bitcast.54, f32[128,768]{1,0:T(8,128)} %get-tuple-element.13, s32[256]{0:T(256)S(1)} %eq.55), kind=kOutput, calls=%fused_computation.16 | convolution fusion | flops 51445760 | bytes 1377280 | tf_op jit(solution)/shard_map/dot_general | solution.py:35
  75.6 1.6 multiply_convert_fusion
  77.1 4.2 %all-to-all-start.4 = ((bf16[768,4,192]{0,2,1:T(8,128)(2,1)}), bf16[768,4,192]{0,2,1:T(8,128)(2,1)S(1)}, u32[]{:S(2)}, u32[]{:S(2)}) async-start(bf16[768,4,192]{0,2,1:T(8,128)(2,1)} %bitcast.52), calls=%async_computation.4 | async-start | bytes 2359296 | tf_op jit(solution)/shard_map/all_to_all | solution.py:168
  81.3 3.1 %collective-permute-start.2 = (bf16[16,768]{1,0:T(8,128)(2,1)S(1)}, bf16[16,768]{1,0:T(8,128)(2,1)S(1)}, u32[]{:S(2)}, u32[]{:S(2)}) collective-permute-start(bf16[16,768]{1,0:T(8,128)(2,1)S(1)} %get-tuple-element.6), channel_id=1, source_target_pairs={{0,1},{1,2},{2,3},{3,4},{4,5},{5,6},{6,7},{8,9},{9,10},{10,11},{11... | collective-permute-start | bytes 73736 | tf_op jit(solution)/shard_map/ppermute | solution.py:19
  84.4 3.7 %collective-permute-start.3 = (bf16[16,768]{1,0:T(8,128)(2,1)S(1)}, bf16[16,768]{1,0:T(8,128)(2,1)S(1)}, u32[]{:S(2)}, u32[]{:S(2)}) collective-permute-start(bf16[16,768]{1,0:T(8,128)(2,1)S(1)} %get-tuple-element.7), channel_id=1, source_target_pairs={{1,0},{2,1},{3,2},{4,3},{5,4},{6,5},{7,6},{9,8},{10,9},{11,10},{12... | collective-permute-start | bytes 73736 | tf_op jit(solution)/shard_map/ppermute | solution.py:21
  88.7 1.4 collective-permute-done.3
  90.1 6.2 %fusion.33 = f32[160,3840]{1,0:T(8,128)} fusion(bf16[3840,768]{1,0:T(8,128)(2,1)} %param.10, bf16[16,768]{1,0:T(8,128)(2,1)S(1)} %collective-permute-done.3, bf16[128,768]{1,0:T(8,128)(2,1)S(1)} %copy-done.3, bf16[16,768]{1,0:T(8,128)(2,1)S(1)} %collective-permute-done.2), kind=kOutput, calls=%fused_computation.70 | convolution fusion | flops 944455680 | bytes 8601600 | tf_op jit(solution)/shard_map/dot_general | solution.py:127
  97.0 0.8 copy.17
  97.8 6.8 %all-to-all-start.5 = ((bf16[8,96,192]{1,2,0:T(8,128)(2,1)}), bf16[8,96,192]{1,2,0:T(8,128)(2,1)S(1)}, u32[]{:S(2)}, u32[]{:S(2)}) async-start(bf16[8,96,192]{1,2,0:T(8,128)(2,1)} %copy.17), calls=%async_computation.5 | async-start | bytes 786432 | tf_op jit(solution)/shard_map/all_to_all | solution.py:172
  104.6 3.4 %pad_dynamic-slice_fusion.2 = (bf16[1024,768]{1,0:T(8,128)(2,1)S(1)}, bf16[1024,768]{1,0:T(8,128)(2,1)}) fusion(s32[]{:T(128)S(6)} %select_n.58, bf16[1024,768]{1,0:T(8,128)(2,1)} %all-gather.3.cloned.1.call-done, s32[]{:T(128)S(6)} %select_n.57), kind=kLoop, calls=%fused_computation.10 | loop fusion | bytes 4718600 | tf_op jit(solution)/shard_map/dynamic_slice | solution.py:152
  108.0 17.3 %all-gather.5.cloned.1.call-done = bf16[1024,768]{1,0:T(8,128)(2,1)} async-done(((bf16[128,768]{1,0:T(8,128)(2,1)}), bf16[1024,768]{1,0:T(8,128)(2,1)}) %all-gather.5.cloned.1.call-update) | async-done | bytes 1572880 | tf_op jit(solution)/shard_map/all_gather | solution.py:157
  125.3 4.6 %multiply_convert_fusion.1 = bf16[576,768]{1,0:T(8,128)(2,1)} fusion(bf16[1024,768]{1,0:T(8,128)(2,1)} %all-gather.5.cloned.1.call-done, s32[]{:T(128)S(6)} %select_n.60, bf16[1024,768]{1,0:T(8,128)(2,1)} %get-tuple-element.5, bf16[1024,768]{1,0:T(8,128)(2,1)S(1)} %get-tuple-element.4), kind=kOutput, calls=%fused_computation.9 | convolution fusion | flops 909213696 | bytes 5603332 | tf_op jit(solution)/shard_map/dot_general | solution.py:35
  129.9 2.2 %copy.16 = bf16[576,768]{0,1:T(8,128)(2,1)} copy(bf16[576,768]{1,0:T(8,128)(2,1)} %multiply_convert_fusion.1) | data formatting | bytes 1769472 | tf_op jit(solution)/shard_map/convert_element_type | solution.py:162
  132.1 3.8 %all-to-all-start.3 = ((bf16[576,4,192]{0,2,1:T(8,128)(2,1)}), bf16[576,4,192]{0,2,1:T(8,128)(2,1)S(1)}, u32[]{:S(2)}, u32[]{:S(2)}) async-start(bf16[576,4,192]{0,2,1:T(8,128)(2,1)} %bitcast.19), calls=%async_computation.3 | async-start | bytes 1966080 | tf_op jit(solution)/shard_map/all_to_all | solution.py:161
  135.9 1.7 %fusion.25 = (f32[128]{0:T(128)S(1)}, f32[128,768]{1,0:T(8,128)S(1)}) fusion(bf16[1,128,768]{2,1,0:T(8,128)(2,1)S(1)} %copy-done.2, f32[160,3840]{1,0:T(8,128)} %fusion.33), kind=kLoop, calls=%fused_computation.49 | loop fusion | flops 688000 | bytes 2556416 | tf_op jit(solution)/shard_map/reduce_sum | solution.py:140
  137.7 0.7 collective-permute-start.4
  138.4 0.7 collective-permute-start.5
  139.0 0.7 collective-permute-start.6
  140.4 6.3 %collective-permute-start.8 = (f32[96,192]{0,1:T(8,128)S(1)}, f32[96,192]{0,1:T(8,128)S(1)}, u32[]{:S(2)}, u32[]{:S(2)}) collective-permute-start(f32[96,192]{0,1:T(8,128)S(1)} %convert_reduce_fusion.1), channel_id=1, source_target_pairs={{0,6},{6,7},{8,14},{14,15},{16,22},{22,23},{24,30},{30,31}} | collective-permute-start | bytes 221192 | tf_op jit(solution)/shard_map/ppermute | solution.py:183
  146.7 1.3 collective-permute-start.9
  147.9 0.8 fusion.43
  148.8 2.1 %collective-permute-done.8 = f32[96,192]{0,1:T(8,128)S(1)} collective-permute-done((f32[96,192]{0,1:T(8,128)S(1)}, f32[96,192]{0,1:T(8,128)S(1)}, u32[]{:S(2)}, u32[]{:S(2)}) %collective-permute-start.8) | collective-permute-done | bytes 73760 | tf_op jit(solution)/shard_map/ppermute | solution.py:183
  150.9 5.0 %collective-permute-done.9 = f32[96,192]{0,1:T(8,128)S(1)} collective-permute-done((f32[96,192]{0,1:T(8,128)S(1)}, f32[96,192]{0,1:T(8,128)S(1)}, u32[]{:S(2)}, u32[]{:S(2)}) %collective-permute-start.9) | collective-permute-done | bytes 73760 | tf_op jit(solution)/shard_map/ppermute | solution.py:183
  156.2 0.8 broadcast_select_fusion.1
  (58 shorter events, 5.1 us)
Async XLA Ops:
  7.2 49.9 %copy-start = (bf16[768,768]{1,0:T(8,128)(2,1)S(1)}, bf16[768,768]{1,0:T(8,128)(2,1)}, u32[]{:S(2)}) copy-start(bf16[768,768]{1,0:T(8,128)(2,1)} %param.11) | copy-start | bytes 3538948
  7.2 22.8 %copy-start.2 = (bf16[1,128,768]{2,1,0:T(8,128)(2,1)S(1)}, bf16[1,128,768]{2,1,0:T(8,128)(2,1)}, u32[]{:S(2)}) copy-start(bf16[1,128,768]{2,1,0:T(8,128)(2,1)} %param.9) | copy-start | bytes 589828
  11.5 16.4 %all-to-all-start = ((s32[8,1,32]{2,1,0:T(1,128)}), s32[8,1,32]{2,1,0:T(1,128)S(1)}, u32[]{:S(2)}, u32[]{:S(2)}) async-start(s32[8,1,32]{2,1,0:T(1,128)} %all_to_all.38), calls=%async_computation | async-start | bytes 8192 | tf_op jit(solution)/shard_map/all_to_all | solution.py:92
  17.6 87.1 %all-gather.3.cloned.1.call-start = ((), (), s32[]{:S(2)}) async-start(), calls=%async_computation.6 | async-start | bytes 1769472 | tf_op jit(solution)/shard_map/all_gather | solution.py:67
  20.3 9.9 %copy-start.1 = (bf16[128,768]{1,0:T(8,128)(2,1)S(1)}, bf16[128,768]{1,0:T(8,128)(2,1)}, u32[]{:S(2)}) copy-start(bf16[128,768]{1,0:T(8,128)(2,1)} %fusion.21) | copy-start | bytes 589828
  21.2 6.9 %collective-permute-start = (bf16[16,768]{1,0:T(8,128)(2,1)S(1)}, bf16[16,768]{1,0:T(8,128)(2,1)S(1)}, u32[]{:S(2)}, u32[]{:S(2)}) collective-permute-start(bf16[16,768]{1,0:T(8,128)(2,1)S(1)} %get-tuple-element.9), channel_id=1, source_target_pairs={{0,1},{1,2},{2,3},{3,4},{4,5},{5,6},{6,7},{8,9},{9,10},{10,11},{11... | collective-permute-start | bytes 73736 | tf_op jit(solution)/shard_map/ppermute | solution.py:19
  24.5 5.7 %collective-permute-start.1 = (bf16[16,768]{1,0:T(8,128)(2,1)S(1)}, bf16[16,768]{1,0:T(8,128)(2,1)S(1)}, u32[]{:S(2)}, u32[]{:S(2)}) collective-permute-start(bf16[16,768]{1,0:T(8,128)(2,1)S(1)} %get-tuple-element.8), channel_id=1, source_target_pairs={{1,0},{2,1},{3,2},{4,3},{5,4},{6,5},{7,6},{9,8},{10,9},{11,10},{12... | collective-permute-start | bytes 73736 | tf_op jit(solution)/shard_map/ppermute | solution.py:21
  36.6 6.8 %copy-start.5 = (bf16[768]{0:T(1024)(128)(2,1)S(1)}, bf16[768]{0:T(1024)(128)(2,1)}, u32[]{:S(2)}) copy-start(bf16[768]{0:T(1024)(128)(2,1)} %param.12) | copy-start | bytes 4612
  36.6 6.8 %copy-start.6 = (s32[1,128]{1,0:T(1,128)S(1)}, s32[1,128]{1,0:T(1,128)}, u32[]{:S(2)}) copy-start(s32[1,128]{1,0:T(1,128)} %param.15) | copy-start | bytes 1540
  37.5 18.7 %all-to-all-start.1 = ((bf16[8,32,768]{2,1,0:T(8,128)(2,1)}), bf16[8,32,768]{2,1,0:T(8,128)(2,1)S(1)}, u32[]{:S(2)}, u32[]{:S(2)}) async-start(bf16[8,32,768]{2,1,0:T(8,128)(2,1)} %broadcast_select_fusion), calls=%async_computation.1 | async-start | bytes 786432 | tf_op jit(solution)/shard_map/all_to_all | solution.py:94
  43.5 13.6 %copy-start.7 = (f32[1,128]{1,0:T(1,128)S(1)}, f32[1,128]{1,0:T(1,128)}, u32[]{:S(2)}) copy-start(f32[1,128]{1,0:T(1,128)} %param.14) | copy-start | bytes 1540
  57.5 10.6 %copy-start.4 = (bf16[1,128,768]{2,1,0:T(8,128)(2,1)S(1)}, bf16[1,128,768]{2,1,0:T(8,128)(2,1)}, u32[]{:S(2)}) copy-start(bf16[1,128,768]{2,1,0:T(8,128)(2,1)} %param.13) | copy-start | bytes 589828
  60.0 13.5 %all-to-all-start.2 = ((bf16[8,32,768]{2,1,0:T(8,128)(2,1)}), bf16[8,32,768]{2,1,0:T(8,128)(2,1)S(1)}, u32[]{:S(2)}, u32[]{:S(2)}) async-start(bf16[8,32,768]{2,1,0:T(8,128)(2,1)} %bitcast.16), calls=%async_computation.2 | async-start | bytes 786432 | tf_op jit(solution)/shard_map/all_to_all | solution.py:117
  66.7 58.5 %all-gather.5.cloned.1.call-start = ((), (), s32[]{:S(2)}) async-start(), calls=%async_computation.7 | async-start | bytes 1769472 | tf_op jit(solution)/shard_map/all_gather | solution.py:157
  77.1 4.2 %copy-start.3 = (bf16[128,768]{1,0:T(8,128)(2,1)S(1)}, bf16[128,768]{1,0:T(8,128)(2,1)}, u32[]{:S(2)}) copy-start(bf16[128,768]{1,0:T(8,128)(2,1)} %fusion.3) | copy-start | bytes 589828
  77.1 19.2 %all-to-all-start.4 = ((bf16[768,4,192]{0,2,1:T(8,128)(2,1)}), bf16[768,4,192]{0,2,1:T(8,128)(2,1)S(1)}, u32[]{:S(2)}, u32[]{:S(2)}) async-start(bf16[768,4,192]{0,2,1:T(8,128)(2,1)} %bitcast.52), calls=%async_computation.4 | async-start | bytes 2359296 | tf_op jit(solution)/shard_map/all_to_all | solution.py:168
  81.3 7.4 %collective-permute-start.2 = (bf16[16,768]{1,0:T(8,128)(2,1)S(1)}, bf16[16,768]{1,0:T(8,128)(2,1)S(1)}, u32[]{:S(2)}, u32[]{:S(2)}) collective-permute-start(bf16[16,768]{1,0:T(8,128)(2,1)S(1)} %get-tuple-element.6), channel_id=1, source_target_pairs={{0,1},{1,2},{2,3},{3,4},{4,5},{5,6},{6,7},{8,9},{9,10},{10,11},{11... | collective-permute-start | bytes 73736 | tf_op jit(solution)/shard_map/ppermute | solution.py:19
  84.4 5.7 %collective-permute-start.3 = (bf16[16,768]{1,0:T(8,128)(2,1)S(1)}, bf16[16,768]{1,0:T(8,128)(2,1)S(1)}, u32[]{:S(2)}, u32[]{:S(2)}) collective-permute-start(bf16[16,768]{1,0:T(8,128)(2,1)S(1)} %get-tuple-element.7), channel_id=1, source_target_pairs={{1,0},{2,1},{3,2},{4,3},{5,4},{6,5},{7,6},{9,8},{10,9},{11,10},{12... | collective-permute-start | bytes 73736 | tf_op jit(solution)/shard_map/ppermute | solution.py:21
  97.8 34.3 %all-to-all-start.5 = ((bf16[8,96,192]{1,2,0:T(8,128)(2,1)}), bf16[8,96,192]{1,2,0:T(8,128)(2,1)S(1)}, u32[]{:S(2)}, u32[]{:S(2)}) async-start(bf16[8,96,192]{1,2,0:T(8,128)(2,1)} %copy.17), calls=%async_computation.5 | async-start | bytes 786432 | tf_op jit(solution)/shard_map/all_to_all | solution.py:172
  132.1 24.0 %all-to-all-start.3 = ((bf16[576,4,192]{0,2,1:T(8,128)(2,1)}), bf16[576,4,192]{0,2,1:T(8,128)(2,1)S(1)}, u32[]{:S(2)}, u32[]{:S(2)}) async-start(bf16[576,4,192]{0,2,1:T(8,128)(2,1)} %bitcast.19), calls=%async_computation.3 | async-start | bytes 1966080 | tf_op jit(solution)/shard_map/all_to_all | solution.py:161
  137.7 9.0 %collective-permute-start.4 = (f32[96,192]{0,1:T(8,128)S(1)}, f32[96,192]{0,1:T(8,128)S(1)}, u32[]{:S(2)}, u32[]{:S(2)}) collective-permute-start(f32[96,192]{0,1:T(8,128)S(1)} %convert_reduce_fusion.1), channel_id=1, source_target_pairs={{2,7},{10,15},{18,23},{26,31}} | collective-permute-start | bytes 221192 | tf_op jit(solution)/shard_map/ppermute | solution.py:183
  138.4 10.4 %collective-permute-start.5 = (f32[96,192]{0,1:T(8,128)S(1)}, f32[96,192]{0,1:T(8,128)S(1)}, u32[]{:S(2)}, u32[]{:S(2)}) collective-permute-start(f32[96,192]{0,1:T(8,128)S(1)} %convert_reduce_fusion.1), channel_id=1, source_target_pairs={{3,7},{11,15},{19,23},{27,31}} | collective-permute-start | bytes 221192 | tf_op jit(solution)/shard_map/ppermute | solution.py:183
  139.0 9.8 %collective-permute-start.6 = (f32[96,192]{0,1:T(8,128)S(1)}, f32[96,192]{0,1:T(8,128)S(1)}, u32[]{:S(2)}, u32[]{:S(2)}) collective-permute-start(f32[96,192]{0,1:T(8,128)S(1)} %convert_reduce_fusion.1), channel_id=1, source_target_pairs={{4,7},{12,15},{20,23},{28,31}} | collective-permute-start | bytes 221192 | tf_op jit(solution)/shard_map/ppermute | solution.py:183
  139.7 9.1 %collective-permute-start.7 = (f32[96,192]{0,1:T(8,128)S(1)}, f32[96,192]{0,1:T(8,128)S(1)}, u32[]{:S(2)}, u32[]{:S(2)}) collective-permute-start(f32[96,192]{0,1:T(8,128)S(1)} %convert_reduce_fusion.1), channel_id=1, source_target_pairs={{5,7},{13,15},{21,23},{29,31}} | collective-permute-start | bytes 221192 | tf_op jit(solution)/shard_map/ppermute | solution.py:183
  140.4 10.5 %collective-permute-start.8 = (f32[96,192]{0,1:T(8,128)S(1)}, f32[96,192]{0,1:T(8,128)S(1)}, u32[]{:S(2)}, u32[]{:S(2)}) collective-permute-start(f32[96,192]{0,1:T(8,128)S(1)} %convert_reduce_fusion.1), channel_id=1, source_target_pairs={{0,6},{6,7},{8,14},{14,15},{16,22},{22,23},{24,30},{30,31}} | collective-permute-start | bytes 221192 | tf_op jit(solution)/shard_map/ppermute | solution.py:183
  146.7 9.2 %collective-permute-start.9 = (f32[96,192]{0,1:T(8,128)S(1)}, f32[96,192]{0,1:T(8,128)S(1)}, u32[]{:S(2)}, u32[]{:S(2)}) collective-permute-start(f32[96,192]{0,1:T(8,128)S(1)} %convert_reduce_fusion.1), channel_id=1, source_target_pairs={{1,6},{7,7},{9,14},{15,15},{17,22},{23,23},{25,30},{31,31}} | collective-permute-start | bytes 221192 | tf_op jit(solution)/shard_map/ppermute | solution.py:183
Sparse Core Ops, SparseCore 0:
  21.1 46.4 all-gather.2
  75.7 49.5 all-gather.4

commit v3 on v2

--- a/solution.py
+++ b/solution.py
@@ -39,6 +39,12 @@
 
 def widened(field, reach_rows):
     return with_halo(field, (("seq", 0),), reach_rows)
+
+
+def scaled(rows):
+    values = rows.astype(jnp.float32)
+    inverse = lax.rsqrt(jnp.mean(values * values, axis=1, keepdims=True) + 1e-05)
+    return (values * inverse).astype(jnp.bfloat16)
 
 
 def per_device(
@@ -63,9 +69,8 @@
     capacity = max(2, 2 * pair_count // shards)
     input_values = activations[0].astype(jnp.float32)
     norm_inverse = lax.rsqrt(jnp.mean(input_values * input_values, axis=1, keepdims=True) + 1e-05)
-    normed = (input_values * norm_inverse).astype(jnp.bfloat16)
-    normed_all = lax.all_gather(normed, "seq", axis=0, tiled=True)
-    padded = widened(normed, reach_rows)
+    normed_all = scaled(lax.all_gather(activations[0], "seq", axis=0, tiled=True))
+    padded = scaled(widened(activations[0], reach_rows))
     tap_rows = tap_count * chan_count
     columns = jnp.concatenate(
         [

time: 165 us -> 164 us (level)
  matrix products: 20.8 us -> 17.7 us
  waiting for transfers between devices: 43.5 us -> 46.6 us
    ppermute x2, waiting for transfers between devices: 1.63 us -> 3.77 us  [with_halo(): lax.ppermute(head, axis, [((i + 1) % count, i) for i in range(ends)])]
    unnamed x4 -> x0, other arithmetic: 1.99 us -> none
    dynamic_slice x1, local copies, waits for them, and re-layouts: 3.35 us -> 1.38 us  [per_device(): lax.dynamic_slice_in_dim(gathered, tap_high * DILATION, all_rows, axis=0)]
  transfers between devices with their start and end apart: 18 -> 18, of which waited for: 8 -> 9; matrix products, arithmetic and copies ran while one was open for 26% -> 23% of each run, Pallas kernels for 0% -> 0%
where the time goes in v3:
time: 164 us; the launch traced here: 163 us
  starting transfers between devices  57.1 us (35%)
  waiting for transfers between devices  46.6 us (28%)
  matrix products  17.7 us (11%)
  between operations  14.5 us (9%)
  other arithmetic  13.7 us (8%)
  local copies, waits for them, and re-layouts  13 us (8%)
    all_gather x1, waiting for transfers between devices, per_device(): grad_all = lax.all_gather(preact_grad, 'seq', axis=0, tiled=True)  17.9 us
    all_to_all x1, waiting for transfers between devices, per_device(): lax.all_to_all(picked, 'seq', split_axis=0, concat_axis=0, tiled=True)  11.4 us
    ppermute x6, starting transfers between devices, per_device(): lax.ppermute(head_block, 'seq', [(i, (skipped + i) // per_owner) for i in...  10.2 us
    dot_general x4, matrix products, contract_rows(): lax.dot_general(left_side, right_side, (((0,), (0,)), ((), ())), preferre...  7.58 us
    ppermute x2, starting transfers between devices, with_halo(): lax.ppermute(head, axis, [((i + 1) % count, i) for i in range(ends)])  7.18 us
    all_to_all x1, starting transfers between devices, per_device(): lax.all_to_all(outgoing, 'seq', split_axis=0, concat_axis=0, tiled=True)  7.02 us
    ppermute x6, waiting for transfers between devices, per_device(): lax.ppermute(head_block, 'seq', [(i, (skipped + i) // per_owner) for i in...  6.53 us
    all_to_all x1, starting transfers between devices, per_device(): lax.all_to_all(head_share.astype(jnp.bfloat16), 'seq', split_axis=0, conc...  6.39 us
  transfers between devices with their start and end apart: 18, of which 9 were waited for; matrix products, arithmetic and copies ran while one was open for 23% of the time, Pallas kernels for 0%

profile of v3, /device:TPU:26, one launch (start us, length us, event | category | flops | bytes accessed | tf_op | source)
XLA Modules:
  0.0 162.6 jit_solution(6406377577428238350)
XLA Ops:
  7.2 0.8 fusion.53
  8.2 0.8 select_reduce_fusion
  9.0 0.7 fusion.56
  9.7 1.1 scatter_custom_fusion
  10.8 0.7 all_to_all.38
  11.5 6.1 %all-to-all-start = ((s32[8,1,32]{2,1,0:T(1,128)}), s32[8,1,32]{2,1,0:T(1,128)S(1)}, u32[]{:S(2)}, u32[]{:S(2)}) async-start(s32[8,1,32]{2,1,0:T(1,128)} %all_to_all.38), calls=%async_computation | async-start | bytes 8192 | tf_op jit(solution)/shard_map/all_to_all | solution.py:97
  17.6 0.7 all-gather.6.cloned.1.call-update
  18.3 0.8 slice_bitcast_fusion.1
  19.0 3.4 %collective-permute-start = (bf16[16,768]{1,0:T(8,128)(2,1)S(1)}, bf16[16,768]{1,0:T(8,128)(2,1)S(1)}, u32[]{:S(2)}, u32[]{:S(2)}) collective-permute-start(bf16[16,768]{1,0:T(8,128)(2,1)S(1)} %get-tuple-element.9), channel_id=1, source_target_pairs={{0,1},{1,2},{2,3},{3,4},{4,5},{5,6},{6,7},{8,9},{9,10},{10,11},{11... | collective-permute-start | bytes 73736 | tf_op jit(solution)/shard_map/ppermute | solution.py:19
  22.4 3.4 %collective-permute-start.1 = (bf16[16,768]{1,0:T(8,128)(2,1)S(1)}, bf16[16,768]{1,0:T(8,128)(2,1)S(1)}, u32[]{:S(2)}, u32[]{:S(2)}) collective-permute-start(bf16[16,768]{1,0:T(8,128)(2,1)S(1)} %get-tuple-element.10), channel_id=1, source_target_pairs={{1,0},{2,1},{3,2},{4,3},{5,4},{6,5},{7,6},{9,8},{10,9},{11,10},{12... | collective-permute-start | bytes 73736 | tf_op jit(solution)/shard_map/ppermute | solution.py:21
  25.9 2.2 %collective-permute-done.1 = bf16[16,768]{1,0:T(8,128)(2,1)S(1)} collective-permute-done((bf16[16,768]{1,0:T(8,128)(2,1)S(1)}, bf16[16,768]{1,0:T(8,128)(2,1)S(1)}, u32[]{:S(2)}, u32[]{:S(2)}) %collective-permute-start.1) | collective-permute-done | bytes 24608 | tf_op jit(solution)/shard_map/ppermute | solution.py:21
  28.1 1.1 fusion.6
  29.2 1.1 fusion.7
  30.4 4.4 %fusion.18 = (bf16[128,768]{1,0:T(8,128)(2,1)S(1)}, f32[128,768]{1,0:T(8,128)S(1)}) fusion(bf16[128,3840]{1,0:T(8,128)(2,1)S(1)} %slice_dynamic-update-slice_fusion, bf16[3840,768]{1,0:T(8,128)(2,1)} %param.10), kind=kOutput, calls=%fused_computation.45 | convolution fusion | flops 761364480 | bytes 7471104 | tf_op jit(solution)/shard_map/dot_general | solution.py:82
  34.8 1.2 gather_fusion.1
  36.0 0.9 broadcast_select_fusion
  36.8 6.0 %all-to-all-start.1 = ((bf16[8,32,768]{2,1,0:T(8,128)(2,1)}), bf16[8,32,768]{2,1,0:T(8,128)(2,1)S(1)}, u32[]{:S(2)}, u32[]{:S(2)}) async-start(bf16[8,32,768]{2,1,0:T(8,128)(2,1)} %broadcast_select_fusion), calls=%async_computation.1 | async-start | bytes 786432 | tf_op jit(solution)/shard_map/all_to_all | solution.py:99
  42.9 0.9 gather_fusion
  43.8 11.4 %all-to-all-done.1 = bf16[8,32,768]{2,1,0:T(8,128)(2,1)S(1)} async-done(((bf16[8,32,768]{2,1,0:T(8,128)(2,1)}), bf16[8,32,768]{2,1,0:T(8,128)(2,1)S(1)}, u32[]{:S(2)}, u32[]{:S(2)}) %all-to-all-start.1) | async-done | bytes 393248 | tf_op jit(solution)/shard_map/all_to_all | solution.py:99
  55.2 0.9 gather_fusion.2
  57.0 1.9 %scatter_custom_fusion.1 = bf16[256,768]{1,0:T(8,128)(2,1)} fusion(s32[128]{0:T(128)S(1)} %get-tuple-element.16, f32[128,768]{1,0:T(8,128)S(1)} %fusion.63, bf16[128,768]{1,0:T(8,128)(2,1)S(1)} %gather_fusion, bf16[]{:T(256)} %constant.50.clone.1), kind=kCustom, calls=%fused_computation.85 | custom fusion | flops 294912 | bytes 983042 | tf_op jit(solution)/shard_map/scatter | solution.py:119
  58.9 7.0 %all-to-all-start.2 = ((bf16[8,32,768]{2,1,0:T(8,128)(2,1)}), bf16[8,32,768]{2,1,0:T(8,128)(2,1)S(1)}, u32[]{:S(2)}, u32[]{:S(2)}) async-start(bf16[8,32,768]{2,1,0:T(8,128)(2,1)} %bitcast.17), calls=%async_computation.2 | async-start | bytes 786432 | tf_op jit(solution)/shard_map/all_to_all | solution.py:122
  67.5 5.4 %all-to-all-done.2 = bf16[8,32,768]{2,1,0:T(8,128)(2,1)S(1)} async-done(((bf16[8,32,768]{2,1,0:T(8,128)(2,1)}), bf16[8,32,768]{2,1,0:T(8,128)(2,1)S(1)}, u32[]{:S(2)}, u32[]{:S(2)}) %all-to-all-start.2) | async-done | bytes 393248 | tf_op jit(solution)/shard_map/all_to_all | solution.py:122
  72.9 1.1 fusion.5
  74.0 1.6 multiply_convert_fusion
  75.6 4.2 %all-to-all-start.4 = ((bf16[768,4,192]{0,2,1:T(8,128)(2,1)}), bf16[768,4,192]{0,2,1:T(8,128)(2,1)S(1)}, u32[]{:S(2)}, u32[]{:S(2)}) async-start(bf16[768,4,192]{0,2,1:T(8,128)(2,1)} %bitcast.58), calls=%async_computation.4 | async-start | bytes 2359296 | tf_op jit(solution)/shard_map/all_to_all | solution.py:173
  79.8 2.9 %collective-permute-start.2 = (bf16[16,768]{1,0:T(8,128)(2,1)S(1)}, bf16[16,768]{1,0:T(8,128)(2,1)S(1)}, u32[]{:S(2)}, u32[]{:S(2)}) collective-permute-start(bf16[16,768]{1,0:T(8,128)(2,1)S(1)} %get-tuple-element.7), channel_id=1, source_target_pairs={{0,1},{1,2},{2,3},{3,4},{4,5},{5,6},{6,7},{8,9},{9,10},{10,11},{11... | collective-permute-start | bytes 73736 | tf_op jit(solution)/shard_map/ppermute | solution.py:19
  82.7 3.8 %collective-permute-start.3 = (bf16[16,768]{1,0:T(8,128)(2,1)S(1)}, bf16[16,768]{1,0:T(8,128)(2,1)S(1)}, u32[]{:S(2)}, u32[]{:S(2)}) collective-permute-start(bf16[16,768]{1,0:T(8,128)(2,1)S(1)} %get-tuple-element.8), channel_id=1, source_target_pairs={{1,0},{2,1},{3,2},{4,3},{5,4},{6,5},{7,6},{9,8},{10,9},{11,10},{12... | collective-permute-start | bytes 73736 | tf_op jit(solution)/shard_map/ppermute | solution.py:21
  86.9 1.5 collective-permute-done.3
  88.4 4.8 %fusion.36 = f32[160,3840]{1,0:T(8,128)S(1)} fusion(bf16[3840,768]{1,0:T(8,128)(2,1)} %param.10, bf16[16,768]{1,0:T(8,128)(2,1)S(1)} %collective-permute-done.3, bf16[128,768]{1,0:T(8,128)(2,1)S(1)} %copy-done.3, bf16[16,768]{1,0:T(8,128)(2,1)S(1)} %collective-permute-done.2), kind=kOutput, calls=%fused_computation.77 | convolution fusion | flops 944455680 | bytes 8601600 | tf_op jit(solution)/shard_map/dot_general | solution.py:132
  94.7 0.8 copy.17
  95.5 6.4 %all-to-all-start.5 = ((bf16[8,96,192]{1,2,0:T(8,128)(2,1)}), bf16[8,96,192]{1,2,0:T(8,128)(2,1)}, u32[]{:S(2)}, u32[]{:S(2)}) async-start(bf16[8,96,192]{1,2,0:T(8,128)(2,1)} %copy.17), calls=%async_computation.5 | async-start | bytes 786432 | tf_op jit(solution)/shard_map/all_to_all | solution.py:177
  101.9 1.9 %fusion = f32[1024]{0:T(1024)S(1)} fusion(bf16[1,1024,768]{2,1,0:T(8,128)(2,1)} %all-gather.6.cloned.1.call-done), kind=kLoop, calls=%fused_computation.7 | loop fusion | flops 2358272 | bytes 1576960 | tf_op jit(solution)/shard_map/reduce_sum | solution.py:46
  104.2 1.4 pad_dynamic-slice_fusion.2
  105.5 17.9 %all-gather.4.cloned.1.call-done = bf16[1024,768]{1,0:T(8,128)(2,1)} async-done(((bf16[128,768]{1,0:T(8,128)(2,1)}), bf16[1024,768]{1,0:T(8,128)(2,1)}) %all-gather.4.cloned.1.call-update) | async-done | bytes 1572880 | tf_op jit(solution)/shard_map/all_gather | solution.py:162
  123.5 4.6 %multiply_convert_fusion.1 = bf16[576,768]{1,0:T(8,128)(2,1)} fusion(bf16[1024,768]{1,0:T(8,128)(2,1)} %all-gather.4.cloned.1.call-done, s32[]{:T(128)S(6)} %select_n.60, bf16[1024,768]{1,0:T(8,128)(2,1)} %get-tuple-element.6, bf16[1024,768]{1,0:T(8,128)(2,1)S(1)} %get-tuple-element.5), kind=kOutput, calls=%fused_computation.13 | convolution fusion | flops 909213696 | bytes 5603332 | tf_op jit(solution)/shard_map/dot_general | solution.py:35
  128.1 2.2 %copy.16 = bf16[576,768]{0,1:T(8,128)(2,1)} copy(bf16[576,768]{1,0:T(8,128)(2,1)} %multiply_convert_fusion.1) | data formatting | bytes 1769472 | tf_op jit(solution)/shard_map/convert_element_type | solution.py:167
  130.3 3.8 %all-to-all-start.3 = ((bf16[576,4,192]{0,2,1:T(8,128)(2,1)}), bf16[576,4,192]{0,2,1:T(8,128)(2,1)S(1)}, u32[]{:S(2)}, u32[]{:S(2)}) async-start(bf16[576,4,192]{0,2,1:T(8,128)(2,1)} %bitcast.22), calls=%async_computation.3 | async-start | bytes 1966080 | tf_op jit(solution)/shard_map/all_to_all | solution.py:166
  134.1 1.1 convert_reduce_fusion.1
  135.2 0.7 collective-permute-start.4
  135.9 0.7 collective-permute-start.5
  137.9 6.3 %collective-permute-start.8 = (f32[96,192]{0,1:T(8,128)S(1)}, f32[96,192]{0,1:T(8,128)S(1)}, u32[]{:S(2)}, u32[]{:S(2)}) collective-permute-start(f32[96,192]{0,1:T(8,128)S(1)} %convert_reduce_fusion.1), channel_id=1, source_target_pairs={{0,6},{6,7},{8,14},{14,15},{16,22},{22,23},{24,30},{30,31}} | collective-permute-start | bytes 221192 | tf_op jit(solution)/shard_map/ppermute | solution.py:188
  144.2 1.3 collective-permute-start.9
  145.5 0.8 fusion.42
  146.4 2.1 %collective-permute-done.8 = f32[96,192]{0,1:T(8,128)S(1)} collective-permute-done((f32[96,192]{0,1:T(8,128)S(1)}, f32[96,192]{0,1:T(8,128)S(1)}, u32[]{:S(2)}, u32[]{:S(2)}) %collective-permute-start.8) | collective-permute-done | bytes 73760 | tf_op jit(solution)/shard_map/ppermute | solution.py:188
  149.1 4.5 %collective-permute-done.9 = f32[96,192]{0,1:T(8,128)} collective-permute-done((f32[96,192]{0,1:T(8,128)S(1)}, f32[96,192]{0,1:T(8,128)}, u32[]{:S(2)}, u32[]{:S(2)}) %collective-permute-start.9) | collective-permute-done | bytes 73760 | tf_op jit(solution)/shard_map/ppermute | solution.py:188
  153.5 1.2 concatenate.19
  154.9 0.8 broadcast_select_fusion.1
  (66 shorter events, 7.2 us)
Async XLA Ops:
  7.2 48.9 %copy-start = (bf16[768,768]{1,0:T(8,128)(2,1)S(1)}, bf16[768,768]{1,0:T(8,128)(2,1)}, u32[]{:S(2)}) copy-start(bf16[768,768]{1,0:T(8,128)(2,1)} %param.11) | copy-start | bytes 3538948
  11.5 14.3 %all-to-all-start = ((s32[8,1,32]{2,1,0:T(1,128)}), s32[8,1,32]{2,1,0:T(1,128)S(1)}, u32[]{:S(2)}, u32[]{:S(2)}) async-start(s32[8,1,32]{2,1,0:T(1,128)} %all_to_all.38), calls=%async_computation | async-start | bytes 8192 | tf_op jit(solution)/shard_map/all_to_all | solution.py:97
  17.6 84.3 %all-gather.6.cloned.1.call-start = ((), (), s32[]{:S(2)}) async-start(), calls=%async_computation.7 | async-start | bytes 1769472 | tf_op jit(solution)/shard_map/all_gather | solution.py:72
  19.0 6.9 %collective-permute-start = (bf16[16,768]{1,0:T(8,128)(2,1)S(1)}, bf16[16,768]{1,0:T(8,128)(2,1)S(1)}, u32[]{:S(2)}, u32[]{:S(2)}) collective-permute-start(bf16[16,768]{1,0:T(8,128)(2,1)S(1)} %get-tuple-element.9), channel_id=1, source_target_pairs={{0,1},{1,2},{2,3},{3,4},{4,5},{5,6},{6,7},{8,9},{9,10},{10,11},{11... | collective-permute-start | bytes 73736 | tf_op jit(solution)/shard_map/ppermute | solution.py:19
  22.4 5.7 %collective-permute-start.1 = (bf16[16,768]{1,0:T(8,128)(2,1)S(1)}, bf16[16,768]{1,0:T(8,128)(2,1)S(1)}, u32[]{:S(2)}, u32[]{:S(2)}) collective-permute-start(bf16[16,768]{1,0:T(8,128)(2,1)S(1)} %get-tuple-element.10), channel_id=1, source_target_pairs={{1,0},{2,1},{3,2},{4,3},{5,4},{6,5},{7,6},{9,8},{10,9},{11,10},{12... | collective-permute-start | bytes 73736 | tf_op jit(solution)/shard_map/ppermute | solution.py:21
  36.0 6.9 %copy-start.8 = (bf16[768]{0:T(1024)(128)(2,1)S(1)}, bf16[768]{0:T(1024)(128)(2,1)}, u32[]{:S(2)}) copy-start(bf16[768]{0:T(1024)(128)(2,1)} %param.12) | copy-start | bytes 4612
  36.8 18.3 %all-to-all-start.1 = ((bf16[8,32,768]{2,1,0:T(8,128)(2,1)}), bf16[8,32,768]{2,1,0:T(8,128)(2,1)S(1)}, u32[]{:S(2)}, u32[]{:S(2)}) async-start(bf16[8,32,768]{2,1,0:T(8,128)(2,1)} %broadcast_select_fusion), calls=%async_computation.1 | async-start | bytes 786432 | tf_op jit(solution)/shard_map/all_to_all | solution.py:99
  42.9 13.2 %copy-start.9 = (f32[1,128]{1,0:T(1,128)S(1)}, f32[1,128]{1,0:T(1,128)}, u32[]{:S(2)}) copy-start(f32[1,128]{1,0:T(1,128)} %param.14) | copy-start | bytes 1540
  56.4 10.7 %copy-start.4 = (bf16[1,128,768]{2,1,0:T(8,128)(2,1)S(1)}, bf16[1,128,768]{2,1,0:T(8,128)(2,1)}, u32[]{:S(2)}) copy-start(bf16[1,128,768]{2,1,0:T(8,128)(2,1)} %param.13) | copy-start | bytes 589828
  56.5 10.7 %copy-start.7 = (s32[1,128]{1,0:T(1,128)S(1)}, s32[1,128]{1,0:T(1,128)}, u32[]{:S(2)}) copy-start(s32[1,128]{1,0:T(1,128)} %param.15) | copy-start | bytes 1540
  58.9 14.0 %all-to-all-start.2 = ((bf16[8,32,768]{2,1,0:T(8,128)(2,1)}), bf16[8,32,768]{2,1,0:T(8,128)(2,1)S(1)}, u32[]{:S(2)}, u32[]{:S(2)}) async-start(bf16[8,32,768]{2,1,0:T(8,128)(2,1)} %bitcast.17), calls=%async_computation.2 | async-start | bytes 786432 | tf_op jit(solution)/shard_map/all_to_all | solution.py:122
  65.9 57.6 %all-gather.4.cloned.1.call-start = ((), (), s32[]{:S(2)}) async-start(), calls=%async_computation.6 | async-start | bytes 1769472 | tf_op jit(solution)/shard_map/all_gather | solution.py:162
  75.6 4.2 %copy-start.3 = (bf16[128,768]{1,0:T(8,128)(2,1)S(1)}, bf16[128,768]{1,0:T(8,128)(2,1)}, u32[]{:S(2)}) copy-start(bf16[128,768]{1,0:T(8,128)(2,1)} %fusion.5) | copy-start | bytes 589828
  75.6 18.4 %all-to-all-start.4 = ((bf16[768,4,192]{0,2,1:T(8,128)(2,1)}), bf16[768,4,192]{0,2,1:T(8,128)(2,1)S(1)}, u32[]{:S(2)}, u32[]{:S(2)}) async-start(bf16[768,4,192]{0,2,1:T(8,128)(2,1)} %bitcast.58), calls=%async_computation.4 | async-start | bytes 2359296 | tf_op jit(solution)/shard_map/all_to_all | solution.py:173
  79.8 7.1 %collective-permute-start.2 = (bf16[16,768]{1,0:T(8,128)(2,1)S(1)}, bf16[16,768]{1,0:T(8,128)(2,1)S(1)}, u32[]{:S(2)}, u32[]{:S(2)}) collective-permute-start(bf16[16,768]{1,0:T(8,128)(2,1)S(1)} %get-tuple-element.7), channel_id=1, source_target_pairs={{0,1},{1,2},{2,3},{3,4},{4,5},{5,6},{6,7},{8,9},{9,10},{10,11},{11... | collective-permute-start | bytes 73736 | tf_op jit(solution)/shard_map/ppermute | solution.py:19
  82.7 5.7 %collective-permute-start.3 = (bf16[16,768]{1,0:T(8,128)(2,1)S(1)}, bf16[16,768]{1,0:T(8,128)(2,1)S(1)}, u32[]{:S(2)}, u32[]{:S(2)}) collective-permute-start(bf16[16,768]{1,0:T(8,128)(2,1)S(1)} %get-tuple-element.8), channel_id=1, source_target_pairs={{1,0},{2,1},{3,2},{4,3},{5,4},{6,5},{7,6},{9,8},{10,9},{11,10},{12... | collective-permute-start | bytes 73736 | tf_op jit(solution)/shard_map/ppermute | solution.py:21
  86.6 6.6 %copy-start.2 = (bf16[1,128,768]{2,1,0:T(8,128)(2,1)S(1)}, bf16[1,128,768]{2,1,0:T(8,128)(2,1)}, u32[]{:S(2)}) copy-start(bf16[1,128,768]{2,1,0:T(8,128)(2,1)} %param.9) | copy-start | bytes 589828
  95.5 34.8 %all-to-all-start.5 = ((bf16[8,96,192]{1,2,0:T(8,128)(2,1)}), bf16[8,96,192]{1,2,0:T(8,128)(2,1)}, u32[]{:S(2)}, u32[]{:S(2)}) async-start(bf16[8,96,192]{1,2,0:T(8,128)(2,1)} %copy.17), calls=%async_computation.5 | async-start | bytes 786432 | tf_op jit(solution)/shard_map/all_to_all | solution.py:177
  101.9 1.9 %copy-start.1 = (bf16[1,1024,768]{2,1,0:T(8,128)(2,1)S(1)}, bf16[1,1024,768]{2,1,0:T(8,128)(2,1)}, u32[]{:S(2)}) copy-start(bf16[1,1024,768]{2,1,0:T(8,128)(2,1)} %all-gather.6.cloned.1.call-done) | copy-start | bytes 4718596
  130.3 24.4 %all-to-all-start.3 = ((bf16[576,4,192]{0,2,1:T(8,128)(2,1)}), bf16[576,4,192]{0,2,1:T(8,128)(2,1)S(1)}, u32[]{:S(2)}, u32[]{:S(2)}) async-start(bf16[576,4,192]{0,2,1:T(8,128)(2,1)} %bitcast.22), calls=%async_computation.3 | async-start | bytes 1966080 | tf_op jit(solution)/shard_map/all_to_all | solution.py:166
  135.2 9.0 %collective-permute-start.4 = (f32[96,192]{0,1:T(8,128)S(1)}, f32[96,192]{0,1:T(8,128)S(1)}, u32[]{:S(2)}, u32[]{:S(2)}) collective-permute-start(f32[96,192]{0,1:T(8,128)S(1)} %convert_reduce_fusion.1), channel_id=1, source_target_pairs={{2,7},{10,15},{18,23},{26,31}} | collective-permute-start | bytes 221192 | tf_op jit(solution)/shard_map/ppermute | solution.py:188
  135.9 10.4 %collective-permute-start.5 = (f32[96,192]{0,1:T(8,128)S(1)}, f32[96,192]{0,1:T(8,128)S(1)}, u32[]{:S(2)}, u32[]{:S(2)}) collective-permute-start(f32[96,192]{0,1:T(8,128)S(1)} %convert_reduce_fusion.1), channel_id=1, source_target_pairs={{3,7},{11,15},{19,23},{27,31}} | collective-permute-start | bytes 221192 | tf_op jit(solution)/shard_map/ppermute | solution.py:188
  136.6 9.8 %collective-permute-start.6 = (f32[96,192]{0,1:T(8,128)S(1)}, f32[96,192]{0,1:T(8,128)S(1)}, u32[]{:S(2)}, u32[]{:S(2)}) collective-permute-start(f32[96,192]{0,1:T(8,128)S(1)} %convert_reduce_fusion.1), channel_id=1, source_target_pairs={{4,7},{12,15},{20,23},{28,31}} | collective-permute-start | bytes 221192 | tf_op jit(solution)/shard_map/ppermute | solution.py:188
  137.3 9.1 %collective-permute-start.7 = (f32[96,192]{0,1:T(8,128)S(1)}, f32[96,192]{0,1:T(8,128)S(1)}, u32[]{:S(2)}, u32[]{:S(2)}) collective-permute-start(f32[96,192]{0,1:T(8,128)S(1)} %convert_reduce_fusion.1), channel_id=1, source_target_pairs={{5,7},{13,15},{21,23},{29,31}} | collective-permute-start | bytes 221192 | tf_op jit(solution)/shard_map/ppermute | solution.py:188
  137.9 10.5 %collective-permute-start.8 = (f32[96,192]{0,1:T(8,128)S(1)}, f32[96,192]{0,1:T(8,128)S(1)}, u32[]{:S(2)}, u32[]{:S(2)}) collective-permute-start(f32[96,192]{0,1:T(8,128)S(1)} %convert_reduce_fusion.1), channel_id=1, source_target_pairs={{0,6},{6,7},{8,14},{14,15},{16,22},{22,23},{24,30},{30,31}} | collective-permute-start | bytes 221192 | tf_op jit(solution)/shard_map/ppermute | solution.py:188
  144.2 9.3 %collective-permute-start.9 = (f32[96,192]{0,1:T(8,128)S(1)}, f32[96,192]{0,1:T(8,128)}, u32[]{:S(2)}, u32[]{:S(2)}) collective-permute-start(f32[96,192]{0,1:T(8,128)S(1)} %convert_reduce_fusion.1), channel_id=1, source_target_pairs={{1,6},{7,7},{9,14},{15,15},{17,22},{23,23},{25,30},{31,31}} | collective-permute-start | bytes 221192 | tf_op jit(solution)/shard_map/ppermute | solution.py:188
  146.4 2.1 %copy-start.5 = (f32[96,192]{0,1:T(8,128)}, f32[96,192]{0,1:T(8,128)S(1)}, u32[]{:S(2)}) copy-start(f32[96,192]{0,1:T(8,128)S(1)} %collective-permute-done.7) | copy-start | bytes 221188
  148.4 0.6 copy-start.6
Sparse Core Ops, SparseCore 0:
  20.6 46.5 all-gather.5
  74.1 49.2 all-gather.3
